TPU v7x, 128 devices: a whole 4x4x4 slice. The times are simulated.
128 devices in a mesh: bx: 8 (over z, core), by: 16 (over y, x).
Axes of the slice: x: 4, y: 4, z: 4, core: 2. Of those that a mesh axis runs over, the one named last changes fastest.
Arguments:
- tracer: float32 [16, 1024, 4096], P(None, 'by', 'bx'), may hold values from -6 to 6
- u_east: float32 [16, 1024, 4096], P(None, 'by', 'bx'), may hold values from -1.5 to 1.5
- v_north: float32 [16, 1024, 4096], P(None, 'by', 'bx'), may hold values from -1.5 to 1.5
- kmt: int32 [1024, 4096], P('by', 'bx'), may hold values from 0 to 16, as said below
- dest: int32 [16, 32], P('by', 'bx'), may hold values from -1 to 7, as said below
- dz: float32 [16], replicated, may hold values from 0.02 to 0.12
- wind: float32 [1024, 4096], P('by', 'bx'), may hold values from -6 to 6
Outputs:
- tracer_out: float32 [16, 1024, 4096], P(None, 'by', 'bx')
- barotropic: float32 [2, 1024, 8192], P(None, 'by', 'bx')
Inputs may be any that keep to these rules, and one draw needn't show every extreme that they name: kmt is 0 on the first and last latitude rows and on every cell of a block whose dest is -1. `dest`: the 4 entries of one device that are not -1 are distinct.
All inputs are finite; a program needn't handle non-finite values.
Results may differ from a plain program's by a relative error of at most 0.0001.
Values sent between devices are 32-bit elements; how exact they have to be, the bound alone decides.
A program may use at most 192 MiB of HBM per device.

v0:
```python
import jax
import jax.numpy as jnp
from jax import lax
from jax.sharding import PartitionSpec as P

BS = 128
SUB = 2
ITERS = 4


KAPPA = 0.12
SIGMA = 0.2
OFFSETS = (
    (-1, -1, 0.5),
    (-1, 0, 1.0),
    (-1, 1, 0.5),
    (0, -1, 1.0),
    (0, 1, 1.0),
    (1, -1, 0.5),
    (1, 0, 1.0),
    (1, 1, 0.5),
)


def extended(shard, sides, width):
    for axis, dim in sides:
        count, length = (lax.axis_size(axis), shard.shape[dim])
        up = [(i, (i + 1) % count) for i in range(count)]
        down = [(j, i) for i, j in up]
        last = lax.slice_in_dim(shard, length - width, length, axis=dim)
        first = lax.slice_in_dim(shard, 0, width, axis=dim)
        before = lax.ppermute(last, axis, up)
        after = lax.ppermute(first, axis, down)
        shard = jnp.concatenate([before, shard, after], axis=dim)
    return shard


def advance(field, east, north, wet):
    flux_east = (
        wet[:, :, :-1]
        * wet[:, :, 1:]
        * (
            east[:, :, :-1] * (field[:, :, :-1] + field[:, :, 1:]) * 0.5
            - KAPPA * (field[:, :, 1:] - field[:, :, :-1])
        )
    )
    flux_north = (
        wet[:, :-1, :]
        * wet[:, 1:, :]
        * (
            north[:, :-1, :] * (field[:, :-1, :] + field[:, 1:, :]) * 0.5
            - KAPPA * (field[:, 1:, :] - field[:, :-1, :])
        )
    )
    spread = (
        flux_east[:, 1:-1, 1:]
        - flux_east[:, 1:-1, :-1]
        + (flux_north[:, 1:, 1:-1] - flux_north[:, :-1, 1:-1])
    )
    return field[:, 1:-1, 1:-1] - wet[:, 1:-1, 1:-1] * spread


def coefficients(depth_pad, ocean_pad):
    row_count = depth_pad.shape[0] - 2
    col_count = depth_pad.shape[1] - 2
    center_depth = depth_pad[1:-1, 1:-1]
    center_ocean = ocean_pad[1:-1, 1:-1]
    couplings = []
    diagonal = jnp.full((row_count, col_count), SIGMA, jnp.float32)
    for row_off, col_off, weight in OFFSETS:
        near_depth = depth_pad[
            1 + row_off : 1 + row_off + row_count, 1 + col_off : 1 + col_off + col_count
        ]
        near_ocean = ocean_pad[
            1 + row_off : 1 + row_off + row_count, 1 + col_off : 1 + col_off + col_count
        ]
        coupling = weight * 0.5 * (center_depth + near_depth) * center_ocean * near_ocean
        couplings.append(coupling)
        diagonal = diagonal + coupling
    return (tuple(couplings), diagonal)


def apply_operator(padded, couplings, diagonal):
    row_count, col_count = diagonal.shape
    result = diagonal * padded[1:-1, 1:-1]
    for (row_off, col_off, weight), coupling in zip(OFFSETS, couplings):
        result = (
            result
            - coupling
            * padded[1 + row_off : 1 + row_off + row_count, 1 + col_off : 1 + col_off + col_count]
        )
    return result


def static_fields(u_east, v_north, wet, width):
    stacked = jnp.stack([u_east, v_north, wet])
    beside_all = extended(stacked, (("bx", 3), ("by", 2)), width)
    return (beside_all[0], beside_all[1], beside_all[2])


def tracer_fields(field, width):
    return extended(field, (("bx", 2), ("by", 1)), width)


def on_device(tracer, u_east, v_north, kmt, dest, dz, wind):
    wet = (lax.broadcasted_iota(jnp.int32, tracer.shape, 0) < kmt[None]).astype(jnp.float32)
    width = 1
    east_pad, north_pad, wet_pad_full = static_fields(u_east, v_north, wet, width)
    field = tracer
    for step in range(SUB):
        field = advance(tracer_fields(field, 1), east_pad, north_pad, wet_pad_full)
    depth_pad = jnp.sum(dz[:, None, None] * wet_pad_full, axis=0)
    couplings, diagonal = coefficients(depth_pad, wet_pad_full[0])
    ocean = wet[0]
    rhs = ocean * (wind + jnp.sum(dz[:, None, None] * wet * field, axis=0))
    solution = jnp.zeros_like(rhs)
    residual = rhs

    def precond_norm(first, second):
        return lax.psum(jnp.sum(first * second), ("bx", "by"))

    precond = residual / diagonal
    direction = precond
    norm_now = precond_norm(residual, precond)
    for step in range(ITERS):
        beside_all = extended(direction, (("bx", 1), ("by", 0)), 1)
        image = apply_operator(beside_all, couplings, diagonal)
        alpha = norm_now / lax.psum(jnp.sum(direction * image), ("bx", "by"))
        solution = solution + alpha * direction
        residual = residual - alpha * image
        precond = residual / diagonal
        norm_next = precond_norm(residual, precond)
        direction = precond + norm_next / norm_now * direction
        norm_now = norm_next
    lon_count = lax.axis_size("bx")
    row_count = solution.shape[0]
    pieces = jnp.stack([solution, residual]).reshape(2, row_count, dest.shape[1], BS)
    targets = lax.broadcasted_iota(jnp.int32, (1, 1, lon_count, 1), 2)
    outgoing = jnp.zeros((2, row_count, lon_count, BS), jnp.float32)
    for block in range(dest.shape[1]):
        match = dest[0, block] == targets
        outgoing = outgoing + jnp.where(match, pieces[:, :, block : block + 1, :], 0.0)
    outgoing = outgoing.reshape(2, row_count, lon_count * BS)
    barotropic = lax.all_to_all(outgoing, "bx", split_axis=2, concat_axis=2, tiled=True)
    return (field, barotropic)


def solution(mesh):
    in_specs = (
        P(None, "by", "bx"),
        P(None, "by", "bx"),
        P(None, "by", "bx"),
        P("by", "bx"),
        P("by", "bx"),
        P(),
        P("by", "bx"),
    )
    out_specs = (P(None, "by", "bx"), P(None, "by", "bx"))
    return jax.shard_map(
        on_device, mesh=mesh, in_specs=in_specs, out_specs=out_specs, check_vma=False
    )
```

profile of v0, /device:TPU:1, one launch (start us, length us, event | category | flops | bytes accessed | tf_op | source)
XLA Modules:
  0.0 637.2 jit_solution(18150515597326876605)
XLA Ops:
  3.1 3.0 collective-permute-start.4
  19.2 3.8 collective-permute-start.7
  28.9 5.0 collective-permute-start.3
  36.8 5.6 pad_maximum_fusion
  42.4 3.1 slice_bitcast_fusion.1
  45.4 7.1 %subtract_multiply_fusion.3 = f32[16,66,513]{2,1,0:T(8,128)} fusion(f32[16,66,514]{2,1,0:T(8,128)} %pad_maximum_fusion.1, f32[16,66,514]{2,1,0:T(8,128)} %get-tuple-element.41, f32[16,66,514]{2,1,0:T(8,128)S(1)} %get-tuple-element.43), kind=kLoop, calls=%fused_computation.16 | loop fusion | flops 4333824 | bytes 13001472 | tf_op jit(solution)/shard_map/mul | solution.py:40
  52.5 5.4 subtract_multiply_fusion.2
  57.9 7.8 %fusion.5 = f32[16,64,512]{2,1,0:T(8,128)S(1)} fusion(f32[16,64,512]{2,1,0:T(8,128)} %param.7, f32[16,65,514]{2,1,0:T(8,128)} %subtract_multiply_fusion.2, f32[16,66,513]{2,1,0:T(8,128)} %subtract_multiply_fusion.3, f32[16,66,514]{2,1,0:T(8,128)S(1)} %get-tuple-element.43), kind=kLoop, calls=%fused_computation.25 | loop fusion | flops 2621440 | bytes 14680064 | tf_op jit(solution)/shard_map/sub | solution.py:60
  68.3 5.8 collective-permute-done.8
  77.3 5.8 collective-permute-start.11
  90.6 4.1 multiply_reduce_fusion.1
  100.3 5.4 collective-permute-start.15
  107.7 68.2 %all-reduce = (f32[]{:T(128)}, f32[]{:T(128)}) all-reduce(f32[]{:T(128)} %get-tuple-element.7, f32[]{:T(128)} %get-tuple-element.6), channel_id=1, replica_groups=mesh['bx'=8,'by'=16] {'bx','by'}, use_global_device_ids=true, to_apply=%region_3.0 | all-reduce | flops 2 | bytes 16 | tf_op jit(solution)/shard_map/psum | solution.py:120
  178.0 62.6 %psum.58 = f32[]{:T(128)} all-reduce(f32[]{:T(128)} %get-tuple-element.22), channel_id=1, replica_groups=mesh['bx'=8,'by'=16] {'bx','by'}, use_global_device_ids=true, to_apply=%region_7.0 | all-reduce | flops 1 | bytes 8 | tf_op jit(solution)/shard_map/psum | solution.py:120
  247.2 4.9 collective-permute-start.19
  254.1 66.7 %psum.59 = f32[]{:T(128)} all-reduce(f32[]{:T(128)} %get-tuple-element.20), channel_id=1, replica_groups=mesh['bx'=8,'by'=16] {'bx','by'}, use_global_device_ids=true, to_apply=%region_9.0 | all-reduce | flops 1 | bytes 8 | tf_op jit(solution)/shard_map/psum | solution.py:128
  322.8 62.6 %psum.60 = f32[]{:T(128)} all-reduce(f32[]{:T(128)} %get-tuple-element.17), channel_id=1, replica_groups=mesh['bx'=8,'by'=16] {'bx','by'}, use_global_device_ids=true, to_apply=%region_11.0 | all-reduce | flops 1 | bytes 8 | tf_op jit(solution)/shard_map/psum | solution.py:120
  391.9 4.8 collective-permute-start.23
  398.8 66.8 %psum.61 = f32[]{:T(128)} all-reduce(f32[]{:T(128)} %get-tuple-element.15), channel_id=1, replica_groups=mesh['bx'=8,'by'=16] {'bx','by'}, use_global_device_ids=true, to_apply=%region_13.0 | all-reduce | flops 1 | bytes 8 | tf_op jit(solution)/shard_map/psum | solution.py:128
  467.6 62.6 %psum.62 = f32[]{:T(128)} all-reduce(f32[]{:T(128)} %get-tuple-element.12), channel_id=1, replica_groups=mesh['bx'=8,'by'=16] {'bx','by'}, use_global_device_ids=true, to_apply=%region_15.0 | all-reduce | flops 1 | bytes 8 | tf_op jit(solution)/shard_map/psum | solution.py:120
  536.8 4.8 collective-permute-start.27
  543.7 66.8 %psum.63 = f32[]{:T(128)} all-reduce(f32[]{:T(128)} %get-tuple-element.10), channel_id=1, replica_groups=mesh['bx'=8,'by'=16] {'bx','by'}, use_global_device_ids=true, to_apply=%region_17.0 | all-reduce | flops 1 | bytes 8 | tf_op jit(solution)/shard_map/psum | solution.py:128
  612.8 5.7 fusion.7
  619.6 13.0 %all_to_all.5 = f32[8,1,16384]{2,1,0:T(1,128)S(1)} all-to-all(f32[8,1,16384]{2,1,0:T(1,128)S(1)} %reshape.52), channel_id=1, replica_groups=mesh['bx'=8,'by'=16] {'bx'}, dimensions={0} | all-to-all | bytes 1048576 | tf_op jit(solution)/shard_map/all_to_all | solution.py:144
  (148 shorter events, 74.9 us)
Async XLA Ops:
  3.1 13.5 %collective-permute-start.4 = (f32[16,64,1]{2,1,0:T(8,128)}, f32[16,64,1]{2,1,0:T(8,128)S(1)}, u32[]{:S(2)}, u32[]{:S(2)}) collective-permute-start(f32[16,64,1]{2,1,0:T(8,128)} %get-tuple-element.52), channel_id=1, source_target_pairs={{0,16},{16,32},{32,48},{48,64},{64,80},{80,96},{96,112},{112,0},{1... | collective-permute-start | bytes 12296 | tf_op jit(solution)/shard_map/ppermute | solution.py:32
  6.2 10.5 %collective-permute-start.5 = (f32[16,64,1]{2,1,0:T(8,128)}, f32[16,64,1]{2,1,0:T(8,128)S(1)}, u32[]{:S(2)}, u32[]{:S(2)}) collective-permute-start(f32[16,64,1]{2,1,0:T(8,128)} %get-tuple-element.53), channel_id=1, source_target_pairs={{16,0},{32,16},{48,32},{64,48},{80,64},{96,80},{112,96},{0,112},{1... | collective-permute-start | bytes 12296 | tf_op jit(solution)/shard_map/ppermute | solution.py:33
  11.6 13.2 %collective-permute-start.1 = (f32[3,16,64,1]{2,1,3,0:T(8,128)S(1)}, f32[3,16,64,1]{2,1,3,0:T(8,128)S(1)}, u32[]{:S(2)}, u32[]{:S(2)}) collective-permute-start(f32[3,16,64,1]{2,1,3,0:T(8,128)S(1)} %copy.28), channel_id=1, source_target_pairs={{16,0},{32,16},{48,32},{64,48},{80,64},{96,80},{112,96},{0,112},{1... | collective-permute-start | bytes 36872 | tf_op jit(solution)/shard_map/ppermute | solution.py:33
  15.5 7.5 %collective-permute-start = (f32[3,16,64,1]{2,1,3,0:T(8,128)S(1)}, f32[3,16,64,1]{2,1,3,0:T(8,128)S(1)}, u32[]{:S(2)}, u32[]{:S(2)}) collective-permute-start(f32[3,16,64,1]{2,1,3,0:T(8,128)S(1)} %copy.27), channel_id=1, source_target_pairs={{0,16},{16,32},{32,48},{48,64},{64,80},{80,96},{96,112},{112,0},{1... | collective-permute-start | bytes 36872 | tf_op jit(solution)/shard_map/ppermute | solution.py:32
  17.9 16.0 %collective-permute-start.6 = (f32[16,1,514]{2,1,0:T(1,128)S(1)}, f32[16,1,514]{2,1,0:T(1,128)S(1)}, u32[]{:S(2)}, u32[]{:S(2)}) collective-permute-start(f32[16,1,514]{2,1,0:T(1,128)S(1)} %get-tuple-element.48), channel_id=1, source_target_pairs={{0,1},{1,2},{2,3},{3,4},{4,5},{5,6},{6,7},{7,8},{8,9},{9,10},{10,1... | collective-permute-start | bytes 98696 | tf_op jit(solution)/shard_map/ppermute | solution.py:32
  19.2 14.7 %collective-permute-start.7 = (f32[16,1,514]{2,1,0:T(1,128)S(1)}, f32[16,1,514]{2,1,0:T(1,128)S(1)}, u32[]{:S(2)}, u32[]{:S(2)}) collective-permute-start(f32[16,1,514]{2,1,0:T(1,128)S(1)} %get-tuple-element.49), channel_id=1, source_target_pairs={{1,0},{2,1},{3,2},{4,3},{5,4},{6,5},{7,6},{8,7},{9,8},{10,9},{11,1... | collective-permute-start | bytes 98696 | tf_op jit(solution)/shard_map/ppermute | solution.py:33
  28.8 7.9 %collective-permute-start.2 = (f32[3,16,1,514]{3,2,1,0:T(1,128)S(1)}, f32[3,16,1,514]{3,2,1,0:T(1,128)S(1)}, u32[]{:S(2)}, u32[]{:S(2)}) collective-permute-start(f32[3,16,1,514]{3,2,1,0:T(1,128)S(1)} %get-tuple-element.39), channel_id=1, source_target_pairs={{0,1},{1,2},{2,3},{3,4},{4,5},{5,6},{6,7},{7,8},{8,9},{9,10},{10,1... | collective-permute-start | bytes 296072 | tf_op jit(solution)/shard_map/ppermute | solution.py:32
  28.9 7.8 %collective-permute-start.3 = (f32[3,16,1,514]{3,2,1,0:T(1,128)S(1)}, f32[3,16,1,514]{3,2,1,0:T(1,128)S(1)}, u32[]{:S(2)}, u32[]{:S(2)}) collective-permute-start(f32[3,16,1,514]{3,2,1,0:T(1,128)S(1)} %get-tuple-element.40), channel_id=1, source_target_pairs={{1,0},{2,1},{3,2},{4,3},{5,4},{6,5},{7,6},{8,7},{9,8},{10,9},{11,1... | collective-permute-start | bytes 296072 | tf_op jit(solution)/shard_map/ppermute | solution.py:33
  65.9 8.2 %collective-permute-start.8 = (f32[16,64,1]{2,1,0:T(8,128)S(1)}, f32[16,64,1]{2,1,0:T(8,128)S(1)}, u32[]{:S(2)}, u32[]{:S(2)}) collective-permute-start(f32[16,64,1]{2,1,0:T(8,128)S(1)} %get-tuple-element.50), channel_id=1, source_target_pairs={{0,16},{16,32},{32,48},{48,64},{64,80},{80,96},{96,112},{112,0},{1... | collective-permute-start | bytes 12296 | tf_op jit(solution)/shard_map/ppermute | solution.py:32
  68.0 8.9 %collective-permute-start.9 = (f32[16,64,1]{2,1,0:T(8,128)S(1)}, f32[16,64,1]{2,1,0:T(8,128)S(1)}, u32[]{:S(2)}, u32[]{:S(2)}) collective-permute-start(f32[16,64,1]{2,1,0:T(8,128)S(1)} %get-tuple-element.51), channel_id=1, source_target_pairs={{16,0},{32,16},{48,32},{64,48},{80,64},{96,80},{112,96},{0,112},{1... | collective-permute-start | bytes 12296 | tf_op jit(solution)/shard_map/ppermute | solution.py:33
  77.2 6.7 %collective-permute-start.10 = (f32[16,1,514]{2,1,0:T(1,128)S(1)}, f32[16,1,514]{2,1,0:T(1,128)S(1)}, u32[]{:S(2)}, u32[]{:S(2)}) collective-permute-start(f32[16,1,514]{2,1,0:T(1,128)S(1)} %get-tuple-element.46), channel_id=1, source_target_pairs={{0,1},{1,2},{2,3},{3,4},{4,5},{5,6},{6,7},{7,8},{8,9},{9,10},{10,1... | collective-permute-start | bytes 98696 | tf_op jit(solution)/shard_map/ppermute | solution.py:32
  77.3 6.9 %collective-permute-start.11 = (f32[16,1,514]{2,1,0:T(1,128)S(1)}, f32[16,1,514]{2,1,0:T(1,128)S(1)}, u32[]{:S(2)}, u32[]{:S(2)}) collective-permute-start(f32[16,1,514]{2,1,0:T(1,128)S(1)} %get-tuple-element.47), channel_id=1, source_target_pairs={{1,0},{2,1},{3,2},{4,3},{5,4},{6,5},{7,6},{8,7},{9,8},{10,9},{11,1... | collective-permute-start | bytes 98696 | tf_op jit(solution)/shard_map/ppermute | solution.py:33
  96.8 3.3 collective-permute-start.13
  100.2 6.4 %collective-permute-start.14 = (f32[1,514]{1,0:T(1,128)S(1)}, f32[1,514]{1,0:T(1,128)S(1)}, u32[]{:S(2)}, u32[]{:S(2)}) collective-permute-start(f32[1,514]{1,0:T(1,128)S(1)} %get-tuple-element.72), channel_id=1, source_target_pairs={{0,1},{1,2},{2,3},{3,4},{4,5},{5,6},{6,7},{7,8},{8,9},{9,10},{10,1... | collective-permute-start | bytes 6176 | tf_op jit(solution)/shard_map/ppermute | solution.py:32
  100.3 6.3 collective-permute-start.15
  243.7 3.3 collective-permute-start.17
  247.1 5.8 collective-permute-start.18
  247.2 5.8 collective-permute-start.19
  388.5 3.3 collective-permute-start.21
  391.9 5.8 collective-permute-start.22
  391.9 5.8 collective-permute-start.23
  533.3 3.3 collective-permute-start.25
  536.7 5.8 collective-permute-start.26
  536.8 5.8 collective-permute-start.27
  (23 other events, 138.4 us)
where the time goes:
time: 643 us; the launch traced here: 637 us
  blocking collectives  469 us (73%)
  other arithmetic  65.4 us (10%)
  starting transfers between devices  49.4 us (8%)
  waiting for transfers between devices  22.8 us (4%)
  local copies, waits for them, and re-layouts  19.4 us (3%)
  between operations  10.8 us (2%)
    psum x4, blocking collectives, precond_norm(): return lax.psum(jnp.sum(first * second), ('bx', 'by'))  256 us
    psum x3, blocking collectives, on_device(): alpha = norm_now / lax.psum(jnp.sum(direction * image), ('bx', 'by'))  200 us
    ppermute x14, starting transfers between devices, extended(): after = lax.ppermute(first, axis, down)  36.9 us
    all_to_all x1, blocking collectives, on_device(): lax.all_to_all(outgoing, 'bx', split_axis=2, concat_axis=2, tiled=True)  13 us
  transfers between devices with their start and end apart: 28, of which 16 were waited for; matrix products, arithmetic and copies ran while one was open for 3% of the time, Pallas kernels for 0%

commit v1 on v0

v1 whole, which is shorter than its diff:
```python
import functools

import jax
import jax.numpy as jnp
from jax import lax
from jax.experimental import pallas as pl
from jax.experimental.pallas import tpu as pltpu
from jax.sharding import PartitionSpec as P

BS = 128
ITERS = 4
KAPPA = 0.12
SIGMA = 0.2
CENTRE = 1.0 / 3.0
HALF = 2.0 / 3.0
MESH = pl.DeviceIdType.MESH
ROWS = 64
COLS = 512
XR = ROWS + 8
XC = COLS + 128
STRIPS = ROWS // 8
F32 = jnp.float32
SIDES = ((0, 1), (0, -1), (1, 0), (-1, 0), (1, 1), (-1, 1), (1, -1), (-1, -1))


def strip(r):
    return pl.ds(8 * r, 8)


def rim(ref, side):
    dx, dy = SIDES[side]
    rows = {1: pl.ds(ROWS - 8, 8), -1: pl.ds(0, 8), 0: pl.ds(0, ROWS)}[dy]
    cols = {1: pl.ds(COLS - 128, 128), -1: pl.ds(0, 128), 0: pl.ds(0, COLS)}[dx]
    return ref.at[rows, cols]


def extend(ext, rims):
    from_s, from_n, from_w, from_e, from_sw, from_se, from_nw, from_ne = rims
    low = lax.broadcasted_iota(jnp.int32, (8, COLS), 0) < 4
    ext[ROWS:XR, 0:COLS] = jnp.where(low, from_n[...], from_s[...])
    east = lax.broadcasted_iota(jnp.int32, (ROWS, 128), 1) < 64
    ext[0:ROWS, COLS:XC] = jnp.where(east, from_e[...], from_w[...])
    east8 = lax.broadcasted_iota(jnp.int32, (8, 128), 1) < 64
    low8 = lax.broadcasted_iota(jnp.int32, (8, 128), 0) < 4
    ext[ROWS:XR, COLS:XC] = jnp.where(
        low8,
        jnp.where(east8, from_ne[...], from_nw[...]),
        jnp.where(east8, from_se[...], from_sw[...]),
    )


def spread_rows(get, count):
    sub = lax.broadcasted_iota(jnp.int32, (8, XC), 0)
    x = [get(r) for r in range(count)]
    up = [pltpu.roll(v, 7, 0) for v in x]
    down = [pltpu.roll(v, 1, 0) for v in x]
    out = []
    for r in range(count):
        north = jnp.where(sub == 7, up[(r + 1) % count], up[r])
        south = jnp.where(sub == 0, down[(r - 1) % count], down[r])
        out.append(x[r] + x[r] + (north + south))
    return out


def spread_cols(v):
    return v + v + (pltpu.roll(v, 1, 1) + pltpu.roll(v, XC - 1, 1))


def kernel(
    nx,
    ny,
    levels,
    tracer,
    u_east,
    v_north,
    kmt,
    dest,
    dz,
    wind,
    tracer_out,
    barotropic,
    c_x,
    u_x,
    v_x,
    k_x,
    ke_x,
    kn_x,
    wind_v,
    ae,
    be,
    an,
    bn,
    c1,
    c2,
    rhs,
    depth,
    inv,
    diag,
    basis,
    krim,
    zrim_row,
    zrim_col,
    zrim_corner,
    krim_row,
    krim_col,
    krim_corner,
    up_send,
    dn_send,
    col_send,
    up_recv,
    dn_recv,
    col_recv,
    ne_recv,
    nw_recv,
    se_recv,
    sw_recv,
    part,
    sums_x,
    part2,
    sums_y,
    stage,
    load_sem,
    out_sem,
    ks,
    kr,
    rs,
    rr,
    zs,
    zr,
    xs,
    xr,
    ys,
    yr,
    ds,
    dr,
):
    mx = lax.axis_index("bx")
    my = lax.axis_index("by")

    def peer(dx, dy):
        return (lax.rem(mx + dx + nx, nx), lax.rem(my + dy + ny, ny))

    inner = (slice(None), pl.ds(0, ROWS), pl.ds(0, COLS))
    loads = [
        pltpu.make_async_copy(tracer, c_x.at[inner], load_sem.at[0]),
        pltpu.make_async_copy(u_east, u_x.at[inner], load_sem.at[1]),
        pltpu.make_async_copy(v_north, v_x.at[inner], load_sem.at[2]),
        pltpu.make_async_copy(kmt, k_x.at[pl.ds(0, ROWS), pl.ds(0, COLS)], load_sem.at[3]),
        pltpu.make_async_copy(wind, wind_v, load_sem.at[4]),
    ]
    for copy in loads:
        copy.start()

    barrier = pltpu.get_barrier_semaphore()
    peers = [peer(off, 0) for off in range(1, nx)]
    peers += [peer(0, off) for off in range(1, ny)]
    peers += [peer(dx, dy) for dx, dy in SIDES[4:]]
    for target in peers:
        pl.semaphore_signal(barrier, inc=1, device_id=target, device_id_type=MESH)
    pl.semaphore_wait(barrier, len(peers))

    def remote(src, dst, send, recv, dx, dy):
        return pltpu.make_async_remote_copy(
            src_ref=src, dst_ref=dst, send_sem=send, recv_sem=recv, device_id=peer(dx, dy), device_id_type=MESH
        )

    def rim_refs(row, col, corner):
        return [row.at[0], row.at[1], col.at[0], col.at[1]] + [corner.at[i] for i in range(4)]

    k_rims = rim_refs(krim_row, krim_col, krim_corner)
    k_sends = [remote(rim(kmt, s), k_rims[s], ks.at[s], kr.at[s], *SIDES[s]) for s in range(8)]
    for copy in k_sends:
        copy.start()

    for copy in loads:
        copy.wait()
    lane = lax.broadcasted_iota(jnp.int32, (ROWS, 128), 1)
    west = lane < 64
    group = ((lane + 4) & 127) >> 3
    slot = ((lane + 4) & 7) - 4
    packed = [jnp.zeros((ROWS, 128), F32) for _ in range(3)]
    for k in range(levels):
        up_send[0, k : k + 1, :] = c_x[k, ROWS - 2 : ROWS - 1, 0:COLS]
        up_send[1, k : k + 1, :] = v_x[k, ROWS - 2 : ROWS - 1, 0:COLS]
        up_send[2, k : k + 1, :] = u_x[k, ROWS - 1 : ROWS, 0:COLS]
        up_send[3, k : k + 1, :] = c_x[k, ROWS - 1 : ROWS, 0:COLS]
        up_send[4, k : k + 1, :] = v_x[k, ROWS - 1 : ROWS, 0:COLS]
        dn_send[0, k : k + 1, :] = c_x[k, 1:2, 0:COLS]
        dn_send[1, k : k + 1, :] = v_x[k, 0:1, 0:COLS]
        dn_send[2, k : k + 1, :] = u_x[k, 0:1, 0:COLS]
        dn_send[3, k : k + 1, :] = c_x[k, 0:1, 0:COLS]
    first, last = pl.ds(0, 128), pl.ds(COLS - 128, 128)
    r_sends = [
        remote(up_send, up_recv, rs.at[0], rr.at[0], 0, 1),
        remote(dn_send, dn_recv, rs.at[1], rr.at[1], 0, -1),
        remote(up_send.at[pl.ds(2, 3), :, last], ne_recv, rs.at[2], rr.at[2], 1, 1),
        remote(up_send.at[pl.ds(3, 2), :, first], nw_recv, rs.at[3], rr.at[3], -1, 1),
        remote(dn_send.at[pl.ds(2, 2), :, last], se_recv, rs.at[4], rr.at[4], 1, -1),
        remote(dn_send.at[pl.ds(3, 1), :, first], sw_recv, rs.at[5], rr.at[5], -1, -1),
    ]
    for copy in r_sends:
        copy.start()
    for k in range(levels):
        for i, field in enumerate((c_x, u_x, v_x)):
            ends = jnp.where(west, field[k, 0:ROWS, 0:128], field[k, 0:ROWS, COLS - 128 : COLS])
            if k:
                ends = pltpu.roll(ends, 8 * k, 1)
            packed[i] = jnp.where(group == k, ends, packed[i])
    pu, pv = pltpu.roll(packed[1], 2, 1), pltpu.roll(packed[2], 3, 1)
    col_send[0] = jnp.where(slot < 0, packed[0], jnp.where(slot < 2, pu, pv))
    col_send[1] = jnp.where(slot < 2, packed[0], jnp.where(slot == 2, pu, pv))
    c_sends = [
        remote(col_send.at[0], col_recv.at[0], rs.at[6], rr.at[6], 1, 0),
        remote(col_send.at[1], col_recv.at[1], rs.at[7], rr.at[7], -1, 0),
    ]
    for copy in c_sends:
        copy.start()

    for copy in k_sends:
        copy.wait()
    extend(k_x, k_rims)
    sub = lax.broadcasted_iota(jnp.int32, (8, XC), 0)
    k_up = [pltpu.roll(k_x[strip(r), :], 7, 0) for r in range(STRIPS + 1)]
    for r in range(STRIPS + 1):
        here = k_x[strip(r), :]
        ke_x[strip(r), :] = jnp.minimum(here, pltpu.roll(here, XC - 1, 1))
        kn_x[strip(r), :] = jnp.minimum(here, jnp.where(sub == 7, k_up[(r + 1) % (STRIPS + 1)], k_up[r]))
        total = jnp.zeros((8, XC), F32)
        for k in range(levels):
            total = total + jnp.where(here > k, dz[k], 0.0)
        depth[strip(r), :] = total

    def ocean_of(r):
        return jnp.where(k_x[strip(r), :] > 0, 1.0, 0.0).astype(F32)

    rows_o = spread_rows(ocean_of, STRIPS + 1)
    rows_d = spread_rows(lambda r: depth[strip(r), :], STRIPS + 1)
    for r in range(STRIPS + 1):
        d = depth[strip(r), :]
        o = ocean_of(r)
        total = d * spread_cols(rows_o[r]) + spread_cols(rows_d[r]) - 8.0 * d
        full = SIGMA + 0.25 * o * total
        diag[strip(r), :] = full
        inv[strip(r), :] = o / full

    for copy in r_sends:
        copy.wait()
    for copy in c_sends:
        copy.wait()
    from_w, from_e = col_recv[0], col_recv[1]
    wide = [
        jnp.where(slot < 0, from_w, from_e),
        jnp.where(slot < 0, pltpu.roll(from_w, 126, 1), pltpu.roll(from_e, 126, 1)),
        jnp.where(slot < 0, pltpu.roll(from_w, 125, 1), pltpu.roll(from_e, 125, 1)),
    ]
    west16 = lax.broadcasted_iota(jnp.int32, (levels, 128), 1) < 64
    c_n = jnp.where(west16, sw_recv[0], se_recv[1])
    u_n = se_recv[0]
    c_s = jnp.where(west16, nw_recv[0], ne_recv[1])
    u_s = ne_recv[0]
    v_s = jnp.where(west16, nw_recv[1], ne_recv[2])
    n0, n1, s2, s1 = ROWS, ROWS + 1, XR - 2, XR - 1
    for k in range(levels):
        for i, field in enumerate((c_x, u_x, v_x)):
            field[k, 0:ROWS, COLS:XC] = pltpu.roll(wide[i], 128 - 8 * k, 1) if k else wide[i]
        for field, row, box, idx in (
            (c_x, n0, dn_recv, 3),
            (c_x, n1, dn_recv, 0),
            (c_x, s2, up_recv, 0),
            (c_x, s1, up_recv, 3),
            (u_x, n0, dn_recv, 2),
            (u_x, s1, up_recv, 2),
            (v_x, n0, dn_recv, 1),
            (v_x, s2, up_recv, 1),
            (v_x, s1, up_recv, 4),
        ):
            field[k, row : row + 1, 0:COLS] = box[idx, k : k + 1, :]
        c_x[k, n0 : n0 + 1, COLS:XC] = c_n[k : k + 1]
        u_x[k, n0 : n0 + 1, COLS:XC] = u_n[k : k + 1]
        c_x[k, s1 : s1 + 1, COLS:XC] = c_s[k : k + 1]
        u_x[k, s1 : s1 + 1, COLS:XC] = u_s[k : k + 1]
        v_x[k, s1 : s1 + 1, COLS:XC] = v_s[k : k + 1]

    rhs[...] = wind_v[...]

    def advance(get, put, width, count):
        def north_flux(r, c, up, nxt):
            c_north = jnp.where(sub == 7, nxt, up)
            return an[strip(r), :] * c + bn[strip(r), :] * c_north

        c = [get(r) for r in range(STRIPS + 1)]
        up = [pltpu.roll(v, 7, 0) for v in c]
        flux = north_flux(STRIPS, c[STRIPS], up[STRIPS], up[0])
        below = pltpu.roll(flux, 1, 0)
        for r in range(count):
            flux = north_flux(r, c[r], up[r], up[(r + 1) % (STRIPS + 1)])
            down = pltpu.roll(flux, 1, 0)
            flux_e = ae[strip(r), :] * c[r] + be[strip(r), :] * pltpu.roll(c[r], XC - 1, 1)
            spread = flux_e - pltpu.roll(flux_e, 1, 1)
            spread = spread + (flux - jnp.where(sub == 0, below, down))
            put(r, (c[r] - spread)[:, :width])
            below = down

    def level(k, carry):
        for r in range(STRIPS + 1):
            half_u, half_v = 0.5 * u_x[k, strip(r), :], 0.5 * v_x[k, strip(r), :]
            wet_e, wet_n = ke_x[strip(r), :] > k, kn_x[strip(r), :] > k
            ae[strip(r), :] = jnp.where(wet_e, half_u + KAPPA, 0.0)
            be[strip(r), :] = jnp.where(wet_e, half_u - KAPPA, 0.0)
            an[strip(r), :] = jnp.where(wet_n, half_v + KAPPA, 0.0)
            bn[strip(r), :] = jnp.where(wet_n, half_v - KAPPA, 0.0)

        def put1(r, value):
            c1[strip(r), :] = value

        def put2(r, value):
            c2[k, strip(r), :] = value
            wet = k_x[strip(r), 0:COLS] > k
            rhs[strip(r), :] = rhs[strip(r), :] + jnp.where(wet, dz[k] * value, 0.0)

        advance(lambda r: c_x[k, strip(r), :], put1, XC, STRIPS + 1)
        advance(lambda r: c1[strip(r), :], put2, COLS, STRIPS)
        pltpu.make_async_copy(c2.at[k], tracer_out.at[k], out_sem.at[k]).start()
        return carry

    lax.fori_loop(0, levels, level, 0)

    for r in range(STRIPS):
        start = jnp.where(k_x[strip(r), 0:COLS] > 0, rhs[strip(r), :], 0.0)
        basis[0, strip(r), 0:COLS] = start * inv[strip(r), 0:COLS]
    z_rims = rim_refs(zrim_row, zrim_col, zrim_corner)
    z_sends = [remote(rim(basis.at[0], s), z_rims[s], zs.at[s], zr.at[s], *SIDES[s]) for s in range(8)]
    for copy in z_sends:
        copy.start()
    for copy in z_sends:
        copy.wait()
    extend(basis.at[0], z_rims)

    moments = [jnp.zeros((8, 128), F32) for _ in range(8)]

    def inner_product(i, j):
        total = jnp.zeros((8, 128), F32)
        for r in range(STRIPS):
            product = diag[strip(r), 0:COLS] * basis[i, strip(r), 0:COLS] * basis[j, strip(r), 0:COLS]
            for m in range(COLS // 128):
                total = total + product[:, 128 * m : 128 * (m + 1)]
        return total

    moments[0] = inner_product(0, 0)
    for step in range(ITERS):
        rows_x = spread_rows(lambda r: basis[step, strip(r), :], STRIPS + 1)
        rows_dx = spread_rows(lambda r: depth[strip(r), :] * basis[step, strip(r), :], STRIPS + 1)
        for r in range(STRIPS + 1):
            d, x = depth[strip(r), :], basis[step, strip(r), :]
            image = d * spread_cols(rows_x[r]) + spread_cols(rows_dx[r]) - 8.0 * (d * x)
            scale = (0.25 / HALF) * inv[strip(r), :]
            following = scale * image - (CENTRE / HALF) * x
            if step:
                following = following + following - basis[step - 1, strip(r), :]
            basis[step + 1, strip(r), :] = following
        moments[2 * step + 1] = inner_product(step, step + 1)
        if step < ITERS - 1:
            moments[2 * step + 2] = inner_product(step + 1, step + 1)

    row8 = lax.broadcasted_iota(jnp.int32, (8, 128), 0)
    mine = jnp.zeros((8, 128), F32)
    for m in range(8):
        mine = jnp.where(row8 == m, jnp.sum(moments[m], axis=0, keepdims=True), mine)
    part[...] = mine
    x_sends = [remote(part, sums_x.at[off], xs.at[off], xr.at[off], off, 0) for off in range(1, nx)]
    for copy in x_sends:
        copy.start()
    total = mine
    for off in range(1, nx):
        x_sends[off - 1].wait()
        total = total + sums_x[off]
    part2[...] = total
    y_sends = [remote(part2, sums_y.at[off], ys.at[off], yr.at[off], 0, off) for off in range(1, ny)]
    for copy in y_sends:
        copy.start()
    for off in range(1, ny):
        y_sends[off - 1].wait()
        total = total + sums_y[off]
    total = jnp.sum(total, axis=1, keepdims=True)
    g = [total[m : m + 1, 0:1] for m in range(8)]

    nu = [g[0], g[1]]
    for m in range(2, 8):
        nu.append(g[m] + g[m] - nu[m % 2])
    gram = {}
    for i in range(ITERS):
        for j in range(ITERS + 1):
            gram[i, j] = 0.5 * (nu[i + j] + nu[abs(i - j)]) if i and j else nu[i + j]

    def dot(a, b):
        terms = []
        for i, first_c in enumerate(a):
            inside = None
            for j, second_c in enumerate(b):
                term = gram[min(i, j), max(i, j)] * second_c
                inside = term if inside is None else inside + term
            terms.append(first_c * inside)
        return functools.reduce(lambda p, q: p + q, terms)

    one = jnp.ones((1, 1), F32)
    zero = jnp.zeros((1, 1), F32)
    z, direction, x = [one], [one], [zero] * ITERS
    norm = dot(z, z)
    for step in range(ITERS):
        image = [(1.0 - CENTRE) * v for v in direction] + [zero]
        for i, v in enumerate(direction):
            if i == 0:
                image[1] = image[1] - HALF * v
            else:
                image[i + 1] = image[i + 1] - (0.5 * HALF) * v
                image[i - 1] = image[i - 1] - (0.5 * HALF) * v
        alpha = norm / dot(direction, image)
        for i, v in enumerate(direction):
            x[i] = x[i] + alpha * v
        z = [v - alpha * w for v, w in zip(z + [zero], image)]
        if step < ITERS - 1:
            following = dot(z, z)
            ratio = following / norm
            direction = [v + ratio * w for v, w in zip(z, direction + [zero])]
            norm = following

    for r in range(STRIPS):
        y = [basis[i, strip(r), 0:COLS] for i in range(ITERS + 1)]
        answer = sum(x[i] * y[i] for i in range(ITERS))
        left = diag[strip(r), 0:COLS] * sum(z[i] * y[i] for i in range(ITERS + 1))
        c1[strip(r), 0:COLS] = answer
        ae[strip(r), 0:COLS] = left
    blocks = COLS // BS
    order = sorted(range(nx), key=lambda off: -min(off, nx - off))
    place = pl.ds(pl.multiple_of(mx * BS, BS), BS)
    d_sends = []
    for off in order:
        target = lax.rem(mx + off, nx)
        for f, field in enumerate((c1, ae)):
            chosen = jnp.zeros((ROWS, BS), F32)
            for m in range(blocks):
                chosen = jnp.where(dest[0, m] == target, field[0:ROWS, m * BS : (m + 1) * BS], chosen)
            stage[off, f] = chosen
        if off:
            copy = remote(stage.at[off], barotropic.at[:, :, place], ds.at[off], dr.at[off], off, 0)
        else:
            copy = pltpu.make_async_copy(stage.at[0], barotropic.at[:, :, place], ds.at[0])
        copy.start()
        d_sends.append(copy)
    for copy in d_sends:
        copy.wait()
    for k in range(levels):
        pltpu.make_async_copy(c2.at[k], tracer_out.at[k], out_sem.at[k]).wait()


def on_device(tracer, u_east, v_north, kmt, dest, dz, wind):
    nx, ny = lax.axis_size("bx"), lax.axis_size("by")
    levels = tracer.shape[0]
    ext3 = pltpu.VMEM((levels, XR, XC), F32)
    ext = pltpu.VMEM((XR, XC), F32)
    ext_i = pltpu.VMEM((XR, XC), jnp.int32)
    flat = pltpu.VMEM((ROWS, COLS), F32)

    def rims(dtype):
        return [
            pltpu.VMEM((2, 8, COLS), dtype),
            pltpu.VMEM((2, ROWS, 128), dtype),
            pltpu.VMEM((4, 8, 128), dtype),
        ]

    scratch = [ext3, ext3, ext3, ext_i, ext_i, ext_i, flat, ext, ext, ext, ext, ext]
    scratch += [pltpu.VMEM((levels, ROWS, COLS), F32), flat, ext, ext, ext]
    scratch += [pltpu.VMEM((ITERS + 1, XR, XC), F32), pltpu.VMEM((8, 128), F32)]
    scratch += rims(F32) + rims(jnp.int32)
    scratch += [
        pltpu.VMEM((5, levels, COLS), F32),
        pltpu.VMEM((4, levels, COLS), F32),
        pltpu.VMEM((2, ROWS, 128), F32),
        pltpu.VMEM((5, levels, COLS), F32),
        pltpu.VMEM((4, levels, COLS), F32),
        pltpu.VMEM((2, ROWS, 128), F32),
        pltpu.VMEM((3, levels, 128), F32),
        pltpu.VMEM((2, levels, 128), F32),
        pltpu.VMEM((2, levels, 128), F32),
        pltpu.VMEM((1, levels, 128), F32),
        pltpu.VMEM((8, 128), F32),
        pltpu.VMEM((nx, 8, 128), F32),
        pltpu.VMEM((8, 128), F32),
        pltpu.VMEM((ny, 8, 128), F32),
        pltpu.VMEM((nx, 2, ROWS, BS), F32),
    ]
    counts = [5, levels] + [8] * 6 + [nx, nx, ny, ny, nx, nx]
    scratch += [pltpu.SemaphoreType.DMA((n,)) for n in counts]
    anywhere = pl.BlockSpec(memory_space=pl.ANY)
    scalars = pl.BlockSpec(memory_space=pltpu.SMEM)
    return pl.pallas_call(
        functools.partial(kernel, nx, ny, levels),
        out_shape=(
            jax.ShapeDtypeStruct(tracer.shape, F32),
            jax.ShapeDtypeStruct((2, ROWS, nx * BS), F32),
        ),
        in_specs=[anywhere] * 4 + [scalars] * 2 + [anywhere],
        out_specs=(anywhere, anywhere),
        scratch_shapes=scratch,
        compiler_params=pltpu.CompilerParams(
            collective_id=0, has_side_effects=True, vmem_limit_bytes=48 * 1024 * 1024
        ),
    )(tracer, u_east, v_north, kmt, dest, dz, wind)


def solution(mesh):
    in_specs = (
        P(None, "by", "bx"),
        P(None, "by", "bx"),
        P(None, "by", "bx"),
        P("by", "bx"),
        P("by", "bx"),
        P(),
        P("by", "bx"),
    )
    out_specs = (P(None, "by", "bx"), P(None, "by", "bx"))
    return jax.shard_map(
        on_device, mesh=mesh, in_specs=in_specs, out_specs=out_specs, check_vma=False
    )
```

time: 643 us -> 58 us (0.09)
  blocking collectives: 469 us -> 0 us
  other arithmetic: 65.4 us -> 0 us
  Pallas kernels: 0 us -> 50.3 us
  starting transfers between devices: 49.4 us -> 0 us
  waiting for transfers between devices: 22.8 us -> 0 us
  local copies, waits for them, and re-layouts: 19.4 us -> 6.82 us
  between operations: 10.8 us -> 0.65 us
    psum x7 -> x0, blocking collectives: 456 us -> none  [the longest x4 256 us: precond_norm(): return lax.psum(jnp.sum(first * second), ('bx', 'by'))]
    pallas_call x0 -> x1, Pallas kernels: none -> 50.3 us  [on_device(): pl.pallas_call(functools.partial(kernel, nx, ny, levels), out_shape=(jax....]
    ppermute x28 -> x0, starting transfers between devices: 49.4 us -> none  [the longest x14 36.9 us: extended(): after = lax.ppermute(first, axis, down)]
    ppermute x28 -> x0, waiting for transfers between devices: 22.8 us -> none  [the longest x14 12.4 us: extended(): after = lax.ppermute(first, axis, down)]
    mul x4 -> x0, other arithmetic: 16.8 us -> none  [the longest x2 8.67 us: advance(): wet[:, :, :-1] * wet[:, :, 1:]]
    all_to_all x1 -> x0, blocking collectives: 13 us -> none  [on_device(): lax.all_to_all(outgoing, 'bx', split_axis=2, concat_axis=2, tiled=True)]
    concatenate x7 -> x0, other arithmetic: 10.1 us -> none  [extended(): shard = jnp.concatenate([before, shard, after], axis=dim)]
    reduce_sum x9 -> x0, other arithmetic: 10.1 us -> none  [the longest x1 4.06 us: on_device(): rhs = ocean * (wind + jnp.sum(dz[:, None, None] * wet * field, axis=0))]
  transfers between devices with their start and end apart: 28 -> 0, of which waited for: 16 -> 0; matrix products, arithmetic and copies ran while one was open for 3% -> 0% of each run, Pallas kernels for 0% -> 0%
where the time goes in v1:
time: 58 us; the launch traced here: 57.8 us
  Pallas kernels  50.3 us (87%)
  local copies, waits for them, and re-layouts  6.82 us (12%)
  between operations  0.65 us (1%)
    pallas_call x1, Pallas kernels, on_device(): pl.pallas_call(functools.partial(kernel, nx, ny, levels), out_shape=(jax....  50.3 us
    unnamed x12, local copies, waits for them, and re-layouts  6.82 us

profile of v1, /device:TPU:1, one launch (start us, length us, event | category | flops | bytes accessed | tf_op | source)
XLA Modules:
  0.0 57.8 jit_solution(18375717953881807322)
XLA Ops:
  0.6 0.0 copy-start
  0.6 1.6 %copy-done = f32[16,64,512]{2,1,0:T(8,128)S(1)} copy-done((f32[16,64,512]{2,1,0:T(8,128)S(1)}, f32[16,64,512]{2,1,0:T(8,128)}, u32[]{:S(2)}) %copy-start) | copy-done | bytes 2097176
  2.2 0.0 copy-start.1
  2.2 0.9 %copy-done.1 = s32[64,512]{1,0:T(8,128)S(1)} copy-done((s32[64,512]{1,0:T(8,128)S(1)}, s32[64,512]{1,0:T(8,128)}, u32[]{:S(2)}) %copy-start.1) | copy-done | bytes 131096
  3.1 0.0 copy-start.2
  3.1 0.9 %copy-done.2 = f32[64,512]{1,0:T(8,128)S(1)} copy-done((f32[64,512]{1,0:T(8,128)S(1)}, f32[64,512]{1,0:T(8,128)}, u32[]{:S(2)}) %copy-start.2) | copy-done | bytes 131096
  4.0 0.0 copy-start.3
  4.0 0.7 %copy-done.3 = s32[1,4]{1,0:T(1,128)S(1)} copy-done((s32[1,4]{1,0:T(1,128)S(1)}, s32[1,4]{1,0:T(1,128)}, u32[]{:S(2)}) %copy-start.3) | copy-done | bytes 40
  4.7 0.0 copy-start.4
  4.7 0.7 %copy-done.4 = f32[16]{0:T(128)S(1)} copy-done((f32[16]{0:T(128)S(1)}, f32[16]{0:T(128)}, u32[]{:S(2)}) %copy-start.4) | copy-done | bytes 88
  5.3 50.3 %shard_map.86 = (f32[16,64,512]{2,1,0:T(8,128)S(1)}, f32[2,64,1024]{2,1,0:T(8,128)S(1)}) custom-call(f32[16,64,512]{2,1,0:T(8,128)S(1)} %copy-done, f32[16,64,512]{2,1,0:T(8,128)} %u_east.1, f32[16,64,512]{2,1,0:T(8,128)} %v_north.1, s32[64,512]{1,0:T(8,128)S(1)} %copy-done.1, s32[1,4]{1,0:T(1,128)S(1)} %copy-done.3, f32[16]{0:T(128)S(1)} %copy-done.4, ...), custom_call_target="tpu_custom_call" | custom-call | tf_op jit(solution)/shard_map/pallas_call | solution.py:496
  55.7 1.3 %copy.11 = f32[16,64,512]{2,1,0:T(8,128)} copy(f32[16,64,512]{2,1,0:T(8,128)S(1)} %get-tuple-element.4) | data formatting | bytes 4194304
  57.0 0.8 %copy.12 = f32[2,64,1024]{2,1,0:T(8,128)} copy(f32[2,64,1024]{2,1,0:T(8,128)S(1)} %get-tuple-element.5) | data formatting | bytes 1048576
Async XLA Ops:
  0.6 1.6 %copy-start = (f32[16,64,512]{2,1,0:T(8,128)S(1)}, f32[16,64,512]{2,1,0:T(8,128)}, u32[]{:S(2)}) copy-start(f32[16,64,512]{2,1,0:T(8,128)} %tracer.1) | copy-start | bytes 6291460
  2.2 0.9 %copy-start.1 = (s32[64,512]{1,0:T(8,128)S(1)}, s32[64,512]{1,0:T(8,128)}, u32[]{:S(2)}) copy-start(s32[64,512]{1,0:T(8,128)} %kmt.1) | copy-start | bytes 393220
  3.1 0.9 %copy-start.2 = (f32[64,512]{1,0:T(8,128)S(1)}, f32[64,512]{1,0:T(8,128)}, u32[]{:S(2)}) copy-start(f32[64,512]{1,0:T(8,128)} %wind.1) | copy-start | bytes 393220
  4.0 0.7 %copy-start.3 = (s32[1,4]{1,0:T(1,128)S(1)}, s32[1,4]{1,0:T(1,128)}, u32[]{:S(2)}) copy-start(s32[1,4]{1,0:T(1,128)} %dest.1) | copy-start | bytes 52
  4.7 0.7 %copy-start.4 = (f32[16]{0:T(128)S(1)}, f32[16]{0:T(128)}, u32[]{:S(2)}) copy-start(f32[16]{0:T(128)} %dz.1) | copy-start | bytes 196

commit v2 on v1

v2 whole, which is shorter than its diff:
```python
import functools

import jax
import jax.numpy as jnp
from jax import lax
from jax.experimental import pallas as pl
from jax.experimental.pallas import tpu as pltpu
from jax.sharding import PartitionSpec as P

BS = 128
ITERS = 4
KAPPA = 0.12
SIGMA = 0.2
CENTRE = 1.0 / 3.0
HALF = 2.0 / 3.0
MESH = pl.DeviceIdType.MESH
ROWS = 64
COLS = 512
XR = ROWS + 8
XC = COLS + 128
STRIPS = ROWS // 8
F32 = jnp.float32
SIDES = ((0, 1), (0, -1), (1, 0), (-1, 0), (1, 1), (-1, 1), (1, -1), (-1, -1))


def strip(r):
    return pl.ds(8 * r, 8)


def rim(ref, side):
    dx, dy = SIDES[side]
    rows = {1: pl.ds(ROWS - 8, 8), -1: pl.ds(0, 8), 0: pl.ds(0, ROWS)}[dy]
    cols = {1: pl.ds(COLS - 128, 128), -1: pl.ds(0, 128), 0: pl.ds(0, COLS)}[dx]
    return ref.at[rows, cols]


def extend(ext, rims):
    from_s, from_n, from_w, from_e, from_sw, from_se, from_nw, from_ne = rims
    low = lax.broadcasted_iota(jnp.int32, (8, COLS), 0) < 4
    ext[ROWS:XR, 0:COLS] = jnp.where(low, from_n[...], from_s[...])
    east = lax.broadcasted_iota(jnp.int32, (ROWS, 128), 1) < 64
    ext[0:ROWS, COLS:XC] = jnp.where(east, from_e[...], from_w[...])
    east8 = lax.broadcasted_iota(jnp.int32, (8, 128), 1) < 64
    low8 = lax.broadcasted_iota(jnp.int32, (8, 128), 0) < 4
    ext[ROWS:XR, COLS:XC] = jnp.where(
        low8,
        jnp.where(east8, from_ne[...], from_nw[...]),
        jnp.where(east8, from_se[...], from_sw[...]),
    )


def spread_rows(get, count):
    sub = lax.broadcasted_iota(jnp.int32, (8, XC), 0)
    x = [get(r) for r in range(count)]
    up = [pltpu.roll(v, 7, 0) for v in x]
    down = [pltpu.roll(v, 1, 0) for v in x]
    out = []
    for r in range(count):
        north = jnp.where(sub == 7, up[(r + 1) % count], up[r])
        south = jnp.where(sub == 0, down[(r - 1) % count], down[r])
        out.append(x[r] + x[r] + (north + south))
    return out


def spread_cols(v):
    return v + v + (pltpu.roll(v, 1, 1) + pltpu.roll(v, XC - 1, 1))


def kernel(
    nx,
    ny,
    levels,
    tracer,
    u_east,
    v_north,
    kmt,
    dest_in,
    dz_in,
    wind,
    tracer_out,
    barotropic,
    c0,
    u0,
    v0,
    c1,
    c2,
    k_x,
    ke,
    kn,
    rhs,
    ae,
    be,
    an,
    bn,
    depth,
    inv,
    diag,
    basis,
    answer,
    left,
    dest,
    dz,
    zrim_row,
    zrim_col,
    zrim_corner,
    krim_row,
    krim_col,
    krim_corner,
    up_send,
    dn_send,
    col_send,
    up_recv,
    dn_recv,
    col_recv,
    rows1,
    rows1_recv,
    cols1,
    cols1_recv,
    row_flux,
    part,
    sums_x,
    part2,
    sums_y,
    stage,
    load_sem,
    out_sem,
    ks,
    kr,
    rs,
    rr,
    zs,
    zr,
    xs,
    xr,
    ys,
    yr,
    ds,
    dr,
):
    mx = lax.axis_index("bx")
    my = lax.axis_index("by")
    pending = []

    def peer(dx, dy):
        return (lax.rem(mx + dx + nx, nx), lax.rem(my + dy + ny, ny))

    def send(src, dst, send_sem, recv_sem, dx, dy):
        copy = pltpu.make_async_remote_copy(
            src_ref=src, dst_ref=dst, send_sem=send_sem, recv_sem=recv_sem, device_id=peer(dx, dy), device_id_type=MESH
        )
        copy.start()
        pending.append(copy)
        return copy

    loads = [
        pltpu.make_async_copy(kmt, k_x.at[pl.ds(0, ROWS), pl.ds(0, COLS)], load_sem.at[0]),
        pltpu.make_async_copy(dest_in, dest, load_sem.at[1]),
        pltpu.make_async_copy(dz_in, dz, load_sem.at[2]),
        pltpu.make_async_copy(tracer, c0, load_sem.at[3]),
        pltpu.make_async_copy(u_east, u0, load_sem.at[4]),
        pltpu.make_async_copy(v_north, v0, load_sem.at[5]),
        pltpu.make_async_copy(wind, rhs, load_sem.at[6]),
    ]
    for copy in loads:
        copy.start()

    barrier = pltpu.get_barrier_semaphore()
    peers = [peer(dx, dy) for dx, dy in SIDES]
    peers += [peer(off, 0) for off in range(2, nx - 1)]
    peers += [peer(0, off) for off in range(2, ny - 1)]
    for target in peers:
        pl.semaphore_signal(barrier, inc=1, device_id=target, device_id_type=MESH)

    loads[0].wait()
    sub = lax.broadcasted_iota(jnp.int32, (8, COLS), 0)
    lane_row = lax.broadcasted_iota(jnp.int32, (8, COLS), 1)
    k_up = [pltpu.roll(k_x[strip(r), 0:COLS], 7, 0) for r in range(STRIPS)]
    for r in range(STRIPS):
        here = k_x[strip(r), 0:COLS]
        east = jnp.where(lane_row == COLS - 1, 0, pltpu.roll(here, COLS - 1, 1))
        north = jnp.where(sub == 7, k_up[r + 1] if r + 1 < STRIPS else 0, k_up[r])
        ke[strip(r), :] = jnp.minimum(here, east)
        kn[strip(r), :] = jnp.minimum(here, north)
    for copy in loads[1:]:
        copy.wait()

    lane = lax.broadcasted_iota(jnp.int32, (ROWS, 128), 1)
    west = lane < 64
    group = ((lane + 4) & 127) >> 3
    slot = ((lane + 4) & 7) - 4

    def ends(field, k):
        return jnp.where(west, field[k, :, 0:128], field[k, :, COLS - 128 : COLS])

    def turned(value, lanes):
        return pltpu.roll(value, lanes % 128, 1) if lanes % 128 else value

    packed = jnp.zeros((ROWS, 128), F32)
    for k in range(levels):
        up_send[0, k : k + 1, :] = c0[k, ROWS - 1 : ROWS, :]
        up_send[1, k : k + 1, :] = v0[k, ROWS - 1 : ROWS, :]
        dn_send[k : k + 1, :] = c0[k, 0:1, :]
        both = jnp.where(slot == -2, turned(u0[k, :, COLS - 128 : COLS], 8 * k - 1), turned(ends(c0, k), 8 * k))
        packed = jnp.where(group == k, both, packed)
    col_send[...] = packed
    pl.semaphore_wait(barrier, len(peers))
    from_s = send(up_send, up_recv, rs.at[0], rr.at[0], 0, 1)
    from_n = send(dn_send, dn_recv, rs.at[1], rr.at[1], 0, -1)
    from_w = send(col_send, col_recv.at[0], rs.at[2], rr.at[2], 1, 0)
    from_e = send(col_send, col_recv.at[1], rs.at[3], rr.at[3], -1, 0)

    def rim_refs(row, col, corner):
        return [row.at[0], row.at[1], col.at[0], col.at[1]] + [corner.at[i] for i in range(4)]

    k_rims = rim_refs(krim_row, krim_col, krim_corner)
    k_sends = [send(rim(kmt, s), k_rims[s], ks.at[s], kr.at[s], *SIDES[s]) for s in range(8)]

    def advance(get, k, put):
        def north_flux(r, c, up, nxt):
            return an[k, strip(r), :] * c + bn[k, strip(r), :] * jnp.where(sub == 7, nxt, up)

        below = jnp.zeros((8, COLS), F32)
        c, up = get(0), pltpu.roll(get(0), 7, 0)
        for r in range(STRIPS):
            if r + 1 < STRIPS:
                c_next = get(r + 1)
                up_next = pltpu.roll(c_next, 7, 0)
            flux = north_flux(r, c, up, up_next)
            down = pltpu.roll(flux, 1, 0)
            flux_e = ae[k, strip(r), :] * c + be[k, strip(r), :] * pltpu.roll(c, COLS - 1, 1)
            spread = flux_e - pltpu.roll(flux_e, 1, 1)
            spread = spread + (flux - jnp.where(sub == 0, below, down))
            put(r, c - spread)
            below, c, up = down, c_next, up_next

    def first_step(k, carry):
        for r in range(STRIPS):
            half_u, half_v = 0.5 * u0[k, strip(r), :], 0.5 * v0[k, strip(r), :]
            wet_e, wet_n = ke[strip(r), :] > k, kn[strip(r), :] > k
            ae[k, strip(r), :] = jnp.where(wet_e, half_u + KAPPA, 0.0)
            be[k, strip(r), :] = jnp.where(wet_e, half_u - KAPPA, 0.0)
            an[k, strip(r), :] = jnp.where(wet_n, half_v + KAPPA, 0.0)
            bn[k, strip(r), :] = jnp.where(wet_n, half_v - KAPPA, 0.0)

        def put(r, value):
            c1[k, strip(r), :] = value

        advance(lambda r: c0[k, strip(r), :], k, put)
        return carry

    lax.fori_loop(0, levels, first_step, 0)

    for copy in k_sends:
        copy.wait_recv()
    extend(k_x, k_rims)
    level16 = lax.broadcasted_iota(jnp.int32, (levels, COLS), 0)
    wet_n = jnp.minimum(k_x[ROWS - 1 : ROWS, 0:COLS], k_x[ROWS : ROWS + 1, 0:COLS]) > level16
    wet_s = jnp.minimum(k_x[0:1, 0:COLS], k_x[XR - 1 : XR, 0:COLS]) > level16
    wet_e = jnp.minimum(k_x[0:ROWS, COLS - 1 : COLS], k_x[0:ROWS, COLS : COLS + 1]) > group
    wet_w = jnp.minimum(k_x[0:ROWS, 0:1], k_x[0:ROWS, XC - 1 : XC]) > group

    def face(velocity, here, there, wet):
        half = 0.5 * velocity
        return jnp.where(wet, (half + KAPPA) * here + (half - KAPPA) * there, 0.0)

    def rim_rows(north_row, south_row, own_north, own_south):
        row_flux[0] = face(up_send[1], own_north, north_row, wet_n)
        row_flux[1] = face(up_recv[1], south_row, own_south, wet_s)

    def rim_cols(own, westward, eastward):
        out = face(turned(col_send[...], 1), own, turned(eastward, -1), wet_e)
        into = face(turned(col_recv[0], 2), turned(westward, 1), own, wet_w)
        return jnp.where(slot == -1, -out, jnp.where(slot == 0, into, 0.0))

    for copy in (from_s, from_n, from_w, from_e):
        copy.wait_recv()
    rim_rows(dn_recv[...], up_recv[0], up_send[0], dn_send[...])
    flux_cols = rim_cols(col_send[...], col_recv[0], col_recv[1])

    def correct(field, k, flux):
        change = turned(flux, -8 * k)
        field[k, :, 0:128] = field[k, :, 0:128] + jnp.where(lane == 0, change, 0.0)
        field[k, :, COLS - 128 : COLS] = field[k, :, COLS - 128 : COLS] + jnp.where(lane == 127, change, 0.0)
        field[k, 0:1, :] = field[k, 0:1, :] + row_flux[1, k : k + 1, :]
        field[k, ROWS - 1 : ROWS, :] = field[k, ROWS - 1 : ROWS, :] - row_flux[0, k : k + 1, :]

    packed = jnp.zeros((ROWS, 128), F32)
    for k in range(levels):
        correct(c1, k, flux_cols)
        rows1[0, k : k + 1, :] = c1[k, ROWS - 1 : ROWS, :]
        rows1[1, k : k + 1, :] = c1[k, 0:1, :]
        packed = jnp.where(group == k, turned(ends(c1, k), 8 * k), packed)
    cols1[...] = packed
    from_s = send(rows1.at[0], rows1_recv.at[0], rs.at[4], rr.at[4], 0, 1)
    from_n = send(rows1.at[1], rows1_recv.at[1], rs.at[5], rr.at[5], 0, -1)
    from_w = send(cols1, cols1_recv.at[0], rs.at[6], rr.at[6], 1, 0)
    from_e = send(cols1, cols1_recv.at[1], rs.at[7], rr.at[7], -1, 0)

    def second_step(k, carry):
        def put(r, value):
            c2[k, strip(r), :] = value
            wet = k_x[strip(r), 0:COLS] > k
            rhs[strip(r), :] = rhs[strip(r), :] + jnp.where(wet, dz[k] * value, 0.0)

        advance(lambda r: c1[k, strip(r), :], k, put)
        return carry

    lax.fori_loop(0, levels, second_step, 0)

    subx = lax.broadcasted_iota(jnp.int32, (8, XC), 0)
    for r in range(STRIPS + 1):
        here = k_x[strip(r), :]
        total = jnp.zeros((8, XC), F32)
        for k in range(levels):
            total = total + jnp.where(here > k, dz[k], 0.0)
        depth[strip(r), :] = total

    def ocean_of(r):
        return jnp.where(k_x[strip(r), :] > 0, 1.0, 0.0).astype(F32)

    rows_o = spread_rows(ocean_of, STRIPS + 1)
    rows_d = spread_rows(lambda r: depth[strip(r), :], STRIPS + 1)
    for r in range(STRIPS + 1):
        d = depth[strip(r), :]
        o = ocean_of(r)
        total = d * spread_cols(rows_o[r]) + spread_cols(rows_d[r]) - 8.0 * d
        full = SIGMA + 0.25 * o * total
        diag[strip(r), :] = full
        inv[strip(r), :] = o / full

    for copy in (from_s, from_n, from_w, from_e):
        copy.wait_recv()
    rim_rows(rows1_recv[1], rows1_recv[0], rows1[0], rows1[1])
    flux_cols = rim_cols(cols1[...], cols1_recv[0], cols1_recv[1])
    dz_rows = jnp.zeros((levels, 128), F32)
    dz_cols = jnp.zeros((ROWS, 128), F32)
    for k in range(levels):
        dz_rows = jnp.where(level16[:, 0:128] == k, dz[k], dz_rows)
        dz_cols = jnp.where(group == k, dz[k], dz_cols)
    dz_rows = jnp.concatenate([dz_rows] * (COLS // 128), axis=1)
    weighted = dz_cols * flux_cols
    change_w = jnp.sum(jnp.where(slot == 0, weighted, 0.0), axis=1, keepdims=True)
    change_e = jnp.sum(jnp.where(slot == -1, weighted, 0.0), axis=1, keepdims=True)
    rhs[:, 0:128] = rhs[:, 0:128] + jnp.where(lane == 0, change_w, 0.0)
    rhs[:, COLS - 128 : COLS] = rhs[:, COLS - 128 : COLS] + jnp.where(lane == 127, change_e, 0.0)
    rhs[0:1, :] = rhs[0:1, :] + jnp.sum(dz_rows * row_flux[1], axis=0, keepdims=True)
    rhs[ROWS - 1 : ROWS, :] = rhs[ROWS - 1 : ROWS, :] - jnp.sum(dz_rows * row_flux[0], axis=0, keepdims=True)

    for r in range(STRIPS):
        start = jnp.where(k_x[strip(r), 0:COLS] > 0, rhs[strip(r), :], 0.0)
        basis[0, strip(r), 0:COLS] = start * inv[strip(r), 0:COLS]
    z_rims = rim_refs(zrim_row, zrim_col, zrim_corner)
    z_sends = [send(rim(basis.at[0], s), z_rims[s], zs.at[s], zr.at[s], *SIDES[s]) for s in range(8)]
    for k in range(levels):
        correct(c2, k, flux_cols)
    write = pltpu.make_async_copy(c2, tracer_out, out_sem)
    write.start()
    for copy in z_sends:
        copy.wait_recv()
    extend(basis.at[0], z_rims)

    moments = [jnp.zeros((8, 128), F32) for _ in range(8)]

    def inner_product(i, j):
        total = jnp.zeros((8, 128), F32)
        for r in range(STRIPS):
            product = diag[strip(r), 0:COLS] * basis[i, strip(r), 0:COLS] * basis[j, strip(r), 0:COLS]
            for m in range(COLS // 128):
                total = total + product[:, 128 * m : 128 * (m + 1)]
        return total

    moments[0] = inner_product(0, 0)
    for step in range(ITERS):
        rows_x = spread_rows(lambda r: basis[step, strip(r), :], STRIPS + 1)
        rows_dx = spread_rows(lambda r: depth[strip(r), :] * basis[step, strip(r), :], STRIPS + 1)
        for r in range(STRIPS + 1):
            d, x = depth[strip(r), :], basis[step, strip(r), :]
            image = d * spread_cols(rows_x[r]) + spread_cols(rows_dx[r]) - 8.0 * (d * x)
            scale = (0.25 / HALF) * inv[strip(r), :]
            following = scale * image - (CENTRE / HALF) * x
            if step:
                following = following + following - basis[step - 1, strip(r), :]
            basis[step + 1, strip(r), :] = following
        moments[2 * step + 1] = inner_product(step, step + 1)
        if step < ITERS - 1:
            moments[2 * step + 2] = inner_product(step + 1, step + 1)

    row8 = lax.broadcasted_iota(jnp.int32, (8, 128), 0)
    mine = jnp.zeros((8, 128), F32)
    for m in range(8):
        mine = jnp.where(row8 == m, jnp.sum(moments[m], axis=0, keepdims=True), mine)
    part[...] = mine
    x_sends = [send(part, sums_x.at[off], xs.at[off], xr.at[off], off, 0) for off in range(1, nx)]
    total = mine
    for off in range(1, nx):
        x_sends[off - 1].wait_recv()
        total = total + sums_x[off]
    part2[...] = total
    y_sends = [send(part2, sums_y.at[off], ys.at[off], yr.at[off], 0, off) for off in range(1, ny)]
    for off in range(1, ny):
        y_sends[off - 1].wait_recv()
        total = total + sums_y[off]
    total = jnp.sum(total, axis=1, keepdims=True)
    g = [total[m : m + 1, 0:1] for m in range(8)]

    nu = [g[0], g[1]]
    for m in range(2, 8):
        nu.append(g[m] + g[m] - nu[m % 2])
    gram = {}
    for i in range(ITERS):
        for j in range(ITERS + 1):
            gram[i, j] = 0.5 * (nu[i + j] + nu[abs(i - j)]) if i and j else nu[i + j]

    def dot(a, b):
        terms = []
        for i, first_c in enumerate(a):
            inside = None
            for j, second_c in enumerate(b):
                term = gram[min(i, j), max(i, j)] * second_c
                inside = term if inside is None else inside + term
            terms.append(first_c * inside)
        return functools.reduce(lambda p, q: p + q, terms)

    one = jnp.ones((1, 1), F32)
    zero = jnp.zeros((1, 1), F32)
    z, direction, x = [one], [one], [zero] * ITERS
    norm = dot(z, z)
    for step in range(ITERS):
        image = [(1.0 - CENTRE) * v for v in direction] + [zero]
        for i, v in enumerate(direction):
            if i == 0:
                image[1] = image[1] - HALF * v
            else:
                image[i + 1] = image[i + 1] - (0.5 * HALF) * v
                image[i - 1] = image[i - 1] - (0.5 * HALF) * v
        alpha = norm / dot(direction, image)
        for i, v in enumerate(direction):
            x[i] = x[i] + alpha * v
        z = [v - alpha * w for v, w in zip(z + [zero], image)]
        if step < ITERS - 1:
            following = dot(z, z)
            ratio = following / norm
            direction = [v + ratio * w for v, w in zip(z, direction + [zero])]
            norm = following

    for r in range(STRIPS):
        y = [basis[i, strip(r), 0:COLS] for i in range(ITERS + 1)]
        answer[strip(r), :] = sum(x[i] * y[i] for i in range(ITERS))
        left[strip(r), :] = diag[strip(r), 0:COLS] * sum(z[i] * y[i] for i in range(ITERS + 1))
    blocks = COLS // BS
    order = sorted(range(nx), key=lambda off: -min(off, nx - off))
    place = pl.ds(pl.multiple_of(mx * BS, BS), BS)
    d_sends = []
    for off in order:
        target = lax.rem(mx + off, nx)
        for f, field in enumerate((answer, left)):
            chosen = jnp.zeros((ROWS, BS), F32)
            for m in range(blocks):
                chosen = jnp.where(dest[0, m] == target, field[0:ROWS, m * BS : (m + 1) * BS], chosen)
            stage[off, f] = chosen
        if off:
            d_sends.append(send(stage.at[off], barotropic.at[:, :, place], ds.at[off], dr.at[off], off, 0))
        else:
            own = pltpu.make_async_copy(stage.at[0], barotropic.at[:, :, place], ds.at[0])
            own.start()
    for copy in d_sends:
        copy.wait_recv()
    own.wait()
    write.wait()
    for copy in pending:
        copy.wait_send()


def on_device(tracer, u_east, v_north, kmt, dest, dz, wind):
    nx, ny = lax.axis_size("bx"), lax.axis_size("by")
    levels = tracer.shape[0]
    slab = pltpu.VMEM((levels, ROWS, COLS), F32)
    ext = pltpu.VMEM((XR, XC), F32)
    flat = pltpu.VMEM((ROWS, COLS), F32)
    flat_i = pltpu.VMEM((ROWS, COLS), jnp.int32)
    rows = pltpu.VMEM((levels, COLS), F32)
    rows2 = pltpu.VMEM((2, levels, COLS), F32)
    cols = pltpu.VMEM((ROWS, 128), F32)
    cols2 = pltpu.VMEM((2, ROWS, 128), F32)

    def rims(dtype):
        return [
            pltpu.VMEM((2, 8, COLS), dtype),
            pltpu.VMEM((2, ROWS, 128), dtype),
            pltpu.VMEM((4, 8, 128), dtype),
        ]

    scratch = [slab] * 5 + [pltpu.VMEM((XR, XC), jnp.int32), flat_i, flat_i, flat] + [slab] * 4
    scratch += [ext, ext, ext, pltpu.VMEM((ITERS + 1, XR, XC), F32), flat, flat]
    scratch += [pltpu.SMEM(dest.shape, jnp.int32), pltpu.SMEM(dz.shape, F32)]
    scratch += rims(F32) + rims(jnp.int32)
    scratch += [rows2, rows, cols, rows2, rows, cols2]
    scratch += [rows2, rows2, cols, cols2, rows2]
    scratch += [
        pltpu.VMEM((8, 128), F32),
        pltpu.VMEM((nx, 8, 128), F32),
        pltpu.VMEM((8, 128), F32),
        pltpu.VMEM((ny, 8, 128), F32),
        pltpu.VMEM((nx, 2, ROWS, BS), F32),
    ]
    counts = [7, None] + [8] * 6 + [nx, nx, ny, ny, nx, nx]
    scratch += [pltpu.SemaphoreType.DMA((n,)) if n else pltpu.SemaphoreType.DMA for n in counts]
    anywhere = pl.BlockSpec(memory_space=pl.ANY)
    hbm = pl.BlockSpec(memory_space=pltpu.HBM)
    return pl.pallas_call(
        functools.partial(kernel, nx, ny, levels),
        out_shape=(
            jax.ShapeDtypeStruct(tracer.shape, F32),
            jax.ShapeDtypeStruct((2, ROWS, nx * BS), F32),
        ),
        in_specs=[hbm] * 7,
        out_specs=(anywhere, anywhere),
        scratch_shapes=scratch,
        compiler_params=pltpu.CompilerParams(
            collective_id=0, has_side_effects=True, vmem_limit_bytes=32 * 1024 * 1024
        ),
    )(*[pltpu.with_memory_space_constraint(x, pltpu.HBM) for x in (tracer, u_east, v_north, kmt, dest, dz, wind)])


def solution(mesh):
    in_specs = (
        P(None, "by", "bx"),
        P(None, "by", "bx"),
        P(None, "by", "bx"),
        P("by", "bx"),
        P("by", "bx"),
        P(),
        P("by", "bx"),
    )
    out_specs = (P(None, "by", "bx"), P(None, "by", "bx"))
    return jax.shard_map(
        on_device, mesh=mesh, in_specs=in_specs, out_specs=out_specs, check_vma=False
    )
```

time: 58 us -> 45.1 us (0.78)
  Pallas kernels: 50.3 us -> 42.2 us
  local copies, waits for them, and re-layouts: 6.82 us -> 2.11 us
    pallas_call x1, Pallas kernels: 50.3 us -> 42.2 us  [on_device(): pl.pallas_call(functools.partial(kernel, nx, ny, levels), out_shape=(jax....]
    unnamed x12 -> x2, local copies, waits for them, and re-layouts: 6.82 us -> 2.11 us
where the time goes in v2:
time: 45.1 us; the launch traced here: 45 us
  Pallas kernels  42.2 us (94%)
  local copies, waits for them, and re-layouts  2.11 us (5%)
  between operations  0.64 us (1%)
    pallas_call x1, Pallas kernels, on_device(): pl.pallas_call(functools.partial(kernel, nx, ny, levels), out_shape=(jax....  42.2 us
    unnamed x2, local copies, waits for them, and re-layouts  2.11 us

profile of v2, /device:TPU:1, one launch (start us, length us, event | category | flops | bytes accessed | tf_op | source)
XLA Modules:
  0.0 45.0 jit_solution(8522052154873776958)
XLA Ops:
  0.6 42.2 %shard_map.86 = (f32[16,64,512]{2,1,0:T(8,128)S(1)}, f32[2,64,1024]{2,1,0:T(8,128)S(1)}) custom-call(f32[16,64,512]{2,1,0:T(8,128)} %tracer.1, f32[16,64,512]{2,1,0:T(8,128)} %u_east.1, f32[16,64,512]{2,1,0:T(8,128)} %v_north.1, s32[64,512]{1,0:T(8,128)} %kmt.1, s32[1,4]{1,0:T(1,128)} %dest_in.1, f32[16]{0:T(128)} %dz_in.1, f32[64,512]{1,0:T(8,128)} %wind.1), custom_call_target="tpu_custom_call" | custom-call | tf_op jit(solution)/shard_map/pallas_call | solution.py:510
  42.9 1.3 %copy.11 = f32[16,64,512]{2,1,0:T(8,128)} copy(f32[16,64,512]{2,1,0:T(8,128)S(1)} %get-tuple-element.4) | data formatting | bytes 4194304
  44.2 0.8 %copy.12 = f32[2,64,1024]{2,1,0:T(8,128)} copy(f32[2,64,1024]{2,1,0:T(8,128)S(1)} %get-tuple-element.5) | data formatting | bytes 1048576

commit v3 on v2

--- a/solution.py
+++ b/solution.py
@@ -49,17 +49,22 @@
     )
 
 
-def spread_rows(get, count):
-    sub = lax.broadcasted_iota(jnp.int32, (8, XC), 0)
+def spread_rows(get, count, inner=False):
     x = [get(r) for r in range(count)]
+    sub = lax.broadcasted_iota(jnp.int32, x[0].shape, 0)
     up = [pltpu.roll(v, 7, 0) for v in x]
     down = [pltpu.roll(v, 1, 0) for v in x]
-    out = []
+    out, within = [], []
     for r in range(count):
         north = jnp.where(sub == 7, up[(r + 1) % count], up[r])
         south = jnp.where(sub == 0, down[(r - 1) % count], down[r])
         out.append(x[r] + x[r] + (north + south))
-    return out
+        if r == 0:
+            south = jnp.where(sub == 0, 0.0, down[r])
+        if r == count - 2:
+            north = jnp.where(sub == 7, 0.0, up[r])
+        within.append(x[r] + x[r] + (north + south) if r in (0, count - 2) else out[r])
+    return (out, within) if inner else out
 
 
 def spread_cols(v):
@@ -96,8 +101,6 @@
     inv,
     diag,
     basis,
-    answer,
-    left,
     dest,
     dz,
     zrim_row,
@@ -121,6 +124,14 @@
     sums_x,
     part2,
     sums_y,
+    still_out,
+    still,
+    first_out,
+    slots,
+    edge_rows,
+    edges_out,
+    edges,
+    full,
     stage,
     load_sem,
     out_sem,
@@ -136,6 +147,11 @@
     yr,
     ds,
     dr,
+    fs,
+    fr,
+    es,
+    er,
+    last_sem,
 ):
     mx = lax.axis_index("bx")
     my = lax.axis_index("by")
@@ -152,14 +168,20 @@
         pending.append(copy)
         return copy
 
+    last_cols = (slice(None), slice(None), pl.ds(COLS - 128, 128))
+    other_cols = (slice(None), slice(None), pl.ds(0, COLS - 128))
+    last_rows = (slice(None), pl.ds(ROWS - 8, 8))
+    other_rows = (slice(None), pl.ds(0, ROWS - 8))
     loads = [
         pltpu.make_async_copy(kmt, k_x.at[pl.ds(0, ROWS), pl.ds(0, COLS)], load_sem.at[0]),
         pltpu.make_async_copy(dest_in, dest, load_sem.at[1]),
         pltpu.make_async_copy(dz_in, dz, load_sem.at[2]),
         pltpu.make_async_copy(tracer, c0, load_sem.at[3]),
-        pltpu.make_async_copy(u_east, u0, load_sem.at[4]),
-        pltpu.make_async_copy(v_north, v0, load_sem.at[5]),
-        pltpu.make_async_copy(wind, rhs, load_sem.at[6]),
+        pltpu.make_async_copy(u_east.at[last_cols], u0.at[last_cols], load_sem.at[4]),
+        pltpu.make_async_copy(v_north.at[last_rows], v0.at[last_rows], load_sem.at[5]),
+        pltpu.make_async_copy(u_east.at[other_cols], u0.at[other_cols], load_sem.at[6]),
+        pltpu.make_async_copy(v_north.at[other_rows], v0.at[other_rows], load_sem.at[7]),
+        pltpu.make_async_copy(wind, rhs, load_sem.at[8]),
     ]
     for copy in loads:
         copy.start()
@@ -181,7 +203,7 @@
         north = jnp.where(sub == 7, k_up[r + 1] if r + 1 < STRIPS else 0, k_up[r])
         ke[strip(r), :] = jnp.minimum(here, east)
         kn[strip(r), :] = jnp.minimum(here, north)
-    for copy in loads[1:]:
+    for copy in loads[1:6]:
         copy.wait()
 
     lane = lax.broadcasted_iota(jnp.int32, (ROWS, 128), 1)
@@ -248,6 +270,8 @@
         advance(lambda r: c0[k, strip(r), :], k, put)
         return carry
 
+    for copy in loads[6:]:
+        copy.wait()
     lax.fori_loop(0, levels, first_step, 0)
 
     for copy in k_sends:
@@ -296,17 +320,6 @@
     from_w = send(cols1, cols1_recv.at[0], rs.at[6], rr.at[6], 1, 0)
     from_e = send(cols1, cols1_recv.at[1], rs.at[7], rr.at[7], -1, 0)
 
-    def second_step(k, carry):
-        def put(r, value):
-            c2[k, strip(r), :] = value
-            wet = k_x[strip(r), 0:COLS] > k
-            rhs[strip(r), :] = rhs[strip(r), :] + jnp.where(wet, dz[k] * value, 0.0)
-
-        advance(lambda r: c1[k, strip(r), :], k, put)
-        return carry
-
-    lax.fori_loop(0, levels, second_step, 0)
-
     subx = lax.broadcasted_iota(jnp.int32, (8, XC), 0)
     for r in range(STRIPS + 1):
         here = k_x[strip(r), :]
@@ -324,9 +337,45 @@
         d = depth[strip(r), :]
         o = ocean_of(r)
         total = d * spread_cols(rows_o[r]) + spread_cols(rows_d[r]) - 8.0 * d
-        full = SIGMA + 0.25 * o * total
-        diag[strip(r), :] = full
-        inv[strip(r), :] = o / full
+        whole = SIGMA + 0.25 * o * total
+        diag[strip(r), :] = whole
+        inv[strip(r), :] = o / whole
+
+    blocks = COLS // BS
+
+    def scatter(get, parts, outbox, inbox, ssem, rsem):
+        copies = []
+        for off in sorted(range(nx), key=lambda o: -min(o, nx - o)):
+            target = lax.rem(mx + off, nx)
+            hits = [dest[0, m] == target for m in range(blocks)]
+            here = outbox.at[off] if off else inbox(0)
+            for i in range(parts):
+                chosen = None
+                for m in range(blocks):
+                    piece = get(m, i)
+                    chosen = jnp.where(hits[m], piece, jnp.zeros_like(piece) if chosen is None else chosen)
+                here[i] = chosen
+            if off:
+                copies.append(send(outbox.at[off], inbox(off), ssem.at[off], rsem.at[off], off, 0))
+        return copies
+
+    def block(m):
+        return pl.ds(m * BS, BS)
+
+    still_copies = scatter(
+        lambda m, i: (depth, inv)[i][0:ROWS, block(m)], 2, still_out, lambda off: still.at[off], ds, dr
+    )
+
+    def second_step(k, carry):
+        def put(r, value):
+            c2[k, strip(r), :] = value
+            wet = k_x[strip(r), 0:COLS] > k
+            rhs[strip(r), :] = rhs[strip(r), :] + jnp.where(wet, dz[k] * value, 0.0)
+
+        advance(lambda r: c1[k, strip(r), :], k, put)
+        return carry
+
+    lax.fori_loop(0, levels, second_step, 0)
 
     for copy in (from_s, from_n, from_w, from_e):
         copy.wait_recv()
@@ -351,6 +400,9 @@
         basis[0, strip(r), 0:COLS] = start * inv[strip(r), 0:COLS]
     z_rims = rim_refs(zrim_row, zrim_col, zrim_corner)
     z_sends = [send(rim(basis.at[0], s), z_rims[s], zs.at[s], zr.at[s], *SIDES[s]) for s in range(8)]
+    first_copies = scatter(
+        lambda m, i: basis[0, 0:ROWS, block(m)], 1, first_out, lambda off: slots.at[off, pl.ds(0, 1)], fs, fr
+    )
     for k in range(levels):
         correct(c2, k, flux_cols)
     write = pltpu.make_async_copy(c2, tracer_out, out_sem)
@@ -370,9 +422,13 @@
         return total
 
     moments[0] = inner_product(0, 0)
+    lanex = lax.broadcasted_iota(jnp.int32, (8, XC), 1)
+    first_lane = (lanex & (BS - 1)) == 0
+    lane8 = lanex[:, 0:BS]
+    edge_cols = [jnp.zeros((8, BS), F32) for _ in range(blocks)]
     for step in range(ITERS):
-        rows_x = spread_rows(lambda r: basis[step, strip(r), :], STRIPS + 1)
-        rows_dx = spread_rows(lambda r: depth[strip(r), :] * basis[step, strip(r), :], STRIPS + 1)
+        rows_x, inner_x = spread_rows(lambda r: basis[step, strip(r), :], STRIPS + 1, True)
+        rows_dx, inner_dx = spread_rows(lambda r: depth[strip(r), :] * basis[step, strip(r), :], STRIPS + 1, True)
         for r in range(STRIPS + 1):
             d, x = depth[strip(r), :], basis[step, strip(r), :]
             image = d * spread_cols(rows_x[r]) + spread_cols(rows_dx[r]) - 8.0 * (d * x)
@@ -381,6 +437,19 @@
             if step:
                 following = following + following - basis[step - 1, strip(r), :]
             basis[step + 1, strip(r), :] = following
+            if r < STRIPS:
+                near_x = jnp.where(first_lane, pltpu.roll(inner_x[r], 1, 1), pltpu.roll(inner_x[r], XC - 1, 1))
+                near_dx = jnp.where(first_lane, pltpu.roll(inner_dx[r], 1, 1), pltpu.roll(inner_dx[r], XC - 1, 1))
+                edge = scale * (d * near_x + near_dx)
+                for m in range(blocks):
+                    moved = pltpu.roll(edge[:, m * BS : (m + 1) * BS], 16 * r + 2 * step + 1, 1)
+                    edge_cols[m] = jnp.where((lane8 >> 1) == 8 * r + step, moved, edge_cols[m])
+            else:
+                beyond_x, beyond_dx = spread_cols(x), spread_cols(d * x)
+                for row, out, at in ((ROWS - 1, 0, 0), (0, 7, 1)):
+                    scale = (0.25 / HALF) * inv[row : row + 1, :]
+                    edge = scale * (depth[row : row + 1, :] * beyond_x[out : out + 1] + beyond_dx[out : out + 1])
+                    edge_rows[2 * step + at : 2 * step + at + 1, :] = edge[:, 0:COLS]
         moments[2 * step + 1] = inner_product(step, step + 1)
         if step < ITERS - 1:
             moments[2 * step + 2] = inner_product(step + 1, step + 1)
@@ -391,12 +460,63 @@
         mine = jnp.where(row8 == m, jnp.sum(moments[m], axis=0, keepdims=True), mine)
     part[...] = mine
     x_sends = [send(part, sums_x.at[off], xs.at[off], xr.at[off], off, 0) for off in range(1, nx)]
+    edge_copies = scatter(
+        lambda m, i: edge_cols[m] if i else edge_rows[:, block(m)], 2, edges_out, lambda off: edges.at[off], es, er
+    )
     total = mine
     for off in range(1, nx):
         x_sends[off - 1].wait_recv()
         total = total + sums_x[off]
     part2[...] = total
     y_sends = [send(part2, sums_y.at[off], ys.at[off], yr.at[off], 0, off) for off in range(1, ny)]
+
+    for copy in still_copies + first_copies + edge_copies:
+        copy.wait_recv()
+
+    def repeat(n, carry):
+        sub8 = lax.broadcasted_iota(jnp.int32, (8, BS), 0)
+        zero8 = jnp.zeros((8, BS), F32)
+        sides = (lane8 == 0) | (lane8 == BS - 1)
+
+        def spread(values):
+            up = [pltpu.roll(v, 7, 0) for v in values]
+            down = [pltpu.roll(v, 1, 0) for v in values]
+            out = []
+            for r in range(STRIPS):
+                north = jnp.where(sub8 == 7, up[r + 1] if r + 1 < STRIPS else 0.0, up[r])
+                south = jnp.where(sub8 == 0, down[r - 1] if r else 0.0, down[r])
+                v = values[r] + values[r] + (north + south)
+                east = jnp.where(lane8 == BS - 1, 0.0, pltpu.roll(v, BS - 1, 1))
+                out.append(v + v + (east + jnp.where(lane8 == 0, 0.0, pltpu.roll(v, 1, 1))))
+            return out
+
+        x = [slots[n, 0, strip(r), :] for r in range(STRIPS)]
+        before = [zero8] * STRIPS
+        for step in range(ITERS):
+            dx = [still[n, 0, strip(r), :] * x[r] for r in range(STRIPS)]
+            wide_x, wide_dx = spread(x), spread(dx)
+            after = []
+            for r in range(STRIPS):
+                image = still[n, 0, strip(r), :] * wide_x[r] + wide_dx[r] - 8.0 * dx[r]
+                following = (0.25 / HALF) * still[n, 1, strip(r), :] * image - (CENTRE / HALF) * x[r]
+                around = pltpu.roll(edges[n, 1], BS - (16 * r + 2 * step + 1), 1)
+                following = following + jnp.where(sides, around, 0.0)
+                if r == STRIPS - 1:
+                    following = following + jnp.where(sub8 == 7, edges[n, 0, 2 * step : 2 * step + 1, :], 0.0)
+                if r == 0:
+                    following = following + jnp.where(sub8 == 0, edges[n, 0, 2 * step + 1 : 2 * step + 2, :], 0.0)
+                if step:
+                    following = following + following - before[r]
+                slots[n, step + 1, strip(r), :] = following
+                after.append(following)
+            before, x = x, after
+        for r in range(STRIPS):
+            scaled = still[n, 1, strip(r), :]
+            full[n, strip(r), :] = jnp.where(scaled > 0.0, 1.0 / jnp.where(scaled > 0.0, scaled, 1.0), 0.0)
+        return carry
+
+    lax.fori_loop(0, nx, repeat, 0)
+
     for off in range(1, ny):
         y_sends[off - 1].wait_recv()
         total = total + sums_y[off]
@@ -443,29 +563,18 @@
             direction = [v + ratio * w for v, w in zip(z, direction + [zero])]
             norm = following
 
-    for r in range(STRIPS):
-        y = [basis[i, strip(r), 0:COLS] for i in range(ITERS + 1)]
-        answer[strip(r), :] = sum(x[i] * y[i] for i in range(ITERS))
-        left[strip(r), :] = diag[strip(r), 0:COLS] * sum(z[i] * y[i] for i in range(ITERS + 1))
-    blocks = COLS // BS
-    order = sorted(range(nx), key=lambda off: -min(off, nx - off))
-    place = pl.ds(pl.multiple_of(mx * BS, BS), BS)
-    d_sends = []
-    for off in order:
-        target = lax.rem(mx + off, nx)
-        for f, field in enumerate((answer, left)):
-            chosen = jnp.zeros((ROWS, BS), F32)
-            for m in range(blocks):
-                chosen = jnp.where(dest[0, m] == target, field[0:ROWS, m * BS : (m + 1) * BS], chosen)
-            stage[off, f] = chosen
-        if off:
-            d_sends.append(send(stage.at[off], barotropic.at[:, :, place], ds.at[off], dr.at[off], off, 0))
-        else:
-            own = pltpu.make_async_copy(stage.at[0], barotropic.at[:, :, place], ds.at[0])
-            own.start()
-    for copy in d_sends:
-        copy.wait_recv()
-    own.wait()
+    results = []
+    for n in range(nx):
+        for r in range(STRIPS):
+            y = [slots[n, i, strip(r), :] for i in range(ITERS + 1)]
+            stage[n, 0, strip(r), :] = sum(x[i] * y[i] for i in range(ITERS))
+            stage[n, 1, strip(r), :] = full[n, strip(r), :] * sum(z[i] * y[i] for i in range(ITERS + 1))
+        place = pl.ds(pl.multiple_of(lax.rem(mx - n + nx, nx) * BS, BS), BS)
+        copy = pltpu.make_async_copy(stage.at[n], barotropic.at[:, :, place], last_sem.at[n])
+        copy.start()
+        results.append(copy)
+    for copy in results:
+        copy.wait()
     write.wait()
     for copy in pending:
         copy.wait_send()
@@ -491,7 +600,7 @@
         ]
 
     scratch = [slab] * 5 + [pltpu.VMEM((XR, XC), jnp.int32), flat_i, flat_i, flat] + [slab] * 4
-    scratch += [ext, ext, ext, pltpu.VMEM((ITERS + 1, XR, XC), F32), flat, flat]
+    scratch += [ext, ext, ext, pltpu.VMEM((ITERS + 1, XR, XC), F32)]
     scratch += [pltpu.SMEM(dest.shape, jnp.int32), pltpu.SMEM(dz.shape, F32)]
     scratch += rims(F32) + rims(jnp.int32)
     scratch += [rows2, rows, cols, rows2, rows, cols2]
@@ -502,8 +611,16 @@
         pltpu.VMEM((8, 128), F32),
         pltpu.VMEM((ny, 8, 128), F32),
         pltpu.VMEM((nx, 2, ROWS, BS), F32),
+        pltpu.VMEM((nx, 2, ROWS, BS), F32),
+        pltpu.VMEM((nx, 1, ROWS, BS), F32),
+        pltpu.VMEM((nx, ITERS + 1, ROWS, BS), F32),
+        pltpu.VMEM((8, COLS), F32),
+        pltpu.VMEM((nx, 2, 8, BS), F32),
+        pltpu.VMEM((nx, 2, 8, BS), F32),
+        pltpu.VMEM((nx, ROWS, BS), F32),
+        pltpu.VMEM((nx, 2, ROWS, BS), F32),
     ]
-    counts = [7, None] + [8] * 6 + [nx, nx, ny, ny, nx, nx]
+    counts = [9, None] + [8] * 6 + [nx, nx, ny, ny] + [nx] * 7
     scratch += [pltpu.SemaphoreType.DMA((n,)) if n else pltpu.SemaphoreType.DMA for n in counts]
     anywhere = pl.BlockSpec(memory_space=pl.ANY)
     hbm = pl.BlockSpec(memory_space=pltpu.HBM)

time: 45.1 us -> 40.9 us (0.907)
  Pallas kernels: 42.2 us -> 38 us
    pallas_call x1, Pallas kernels: 42.2 us -> 38 us  [on_device(): pl.pallas_call(functools.partial(kernel, nx, ny, levels), out_shape=(jax....]
where the time goes in v3:
time: 40.9 us; the launch traced here: 40.8 us
  Pallas kernels  38 us (93%)
  local copies, waits for them, and re-layouts  2.11 us (5%)
  between operations  0.64 us (2%)
    pallas_call x1, Pallas kernels, on_device(): pl.pallas_call(functools.partial(kernel, nx, ny, levels), out_shape=(jax....  38 us
    unnamed x2, local copies, waits for them, and re-layouts  2.11 us

profile of v3, /device:TPU:1, one launch (start us, length us, event | category | flops | bytes accessed | tf_op | source)
XLA Modules:
  0.0 40.8 jit_solution(12692691505201461374)
XLA Ops:
  0.6 38.0 %shard_map.86 = (f32[16,64,512]{2,1,0:T(8,128)S(1)}, f32[2,64,1024]{2,1,0:T(8,128)S(1)}) custom-call(f32[16,64,512]{2,1,0:T(8,128)} %tracer.1, f32[16,64,512]{2,1,0:T(8,128)} %u_east.1, f32[16,64,512]{2,1,0:T(8,128)} %v_north.1, s32[64,512]{1,0:T(8,128)} %kmt.1, s32[1,4]{1,0:T(1,128)} %dest_in.1, f32[16]{0:T(128)} %dz_in.1, f32[64,512]{1,0:T(8,128)} %wind.1), custom_call_target="tpu_custom_call" | custom-call | tf_op jit(solution)/shard_map/pallas_call | solution.py:627
  38.7 1.3 %copy.11 = f32[16,64,512]{2,1,0:T(8,128)} copy(f32[16,64,512]{2,1,0:T(8,128)S(1)} %get-tuple-element.4) | data formatting | bytes 4194304
  40.0 0.8 %copy.12 = f32[2,64,1024]{2,1,0:T(8,128)} copy(f32[2,64,1024]{2,1,0:T(8,128)S(1)} %get-tuple-element.5) | data formatting | bytes 1048576

commit v4 on v3

--- a/solution.py
+++ b/solution.py
@@ -34,13 +34,25 @@
     return ref.at[rows, cols]
 
 
+def pack_ends(ext):
+    lane = lax.broadcasted_iota(jnp.int32, (8, 128), 1)
+    packed = jnp.zeros((8, 128), ext.dtype)
+    for r in range(STRIPS):
+        both = jnp.where(lane < 64, ext[strip(r), 0:128], ext[strip(r), COLS - 128 : COLS])
+        both = pltpu.roll(both, 16 * r, 1) if r else both
+        packed = jnp.where(((lane + 8) & 127) >> 4 == r, both, packed)
+    return packed
+
+
 def extend(ext, rims):
     from_s, from_n, from_w, from_e, from_sw, from_se, from_nw, from_ne = rims
     low = lax.broadcasted_iota(jnp.int32, (8, COLS), 0) < 4
     ext[ROWS:XR, 0:COLS] = jnp.where(low, from_n[...], from_s[...])
-    east = lax.broadcasted_iota(jnp.int32, (ROWS, 128), 1) < 64
-    ext[0:ROWS, COLS:XC] = jnp.where(east, from_e[...], from_w[...])
-    east8 = lax.broadcasted_iota(jnp.int32, (8, 128), 1) < 64
+    lane = lax.broadcasted_iota(jnp.int32, (8, 128), 1)
+    ends = jnp.where(((lane + 8) & 15) < 8, from_w[...], from_e[...])
+    for r in range(STRIPS):
+        ext[strip(r), COLS:XC] = pltpu.roll(ends, 128 - 16 * r, 1) if r else ends
+    east8 = lane < 64
     low8 = lax.broadcasted_iota(jnp.int32, (8, 128), 0) < 4
     ext[ROWS:XR, COLS:XC] = jnp.where(
         low8,
@@ -49,22 +61,17 @@
     )
 
 
-def spread_rows(get, count, inner=False):
+def spread_rows(get, count, wrap=True):
     x = [get(r) for r in range(count)]
     sub = lax.broadcasted_iota(jnp.int32, x[0].shape, 0)
     up = [pltpu.roll(v, 7, 0) for v in x]
     down = [pltpu.roll(v, 1, 0) for v in x]
-    out, within = [], []
+    out = []
     for r in range(count):
-        north = jnp.where(sub == 7, up[(r + 1) % count], up[r])
-        south = jnp.where(sub == 0, down[(r - 1) % count], down[r])
+        north = jnp.where(sub == 7, up[(r + 1) % count] if wrap or r + 1 < count else 0.0, up[r])
+        south = jnp.where(sub == 0, down[r - 1] if wrap or r else 0.0, down[r])
         out.append(x[r] + x[r] + (north + south))
-        if r == 0:
-            south = jnp.where(sub == 0, 0.0, down[r])
-        if r == count - 2:
-            north = jnp.where(sub == 7, 0.0, up[r])
-        within.append(x[r] + x[r] + (north + south) if r in (0, count - 2) else out[r])
-    return (out, within) if inner else out
+    return out
 
 
 def spread_cols(v):
@@ -119,6 +126,10 @@
     rows1_recv,
     cols1,
     cols1_recv,
+    rows_own,
+    cols_own,
+    kends,
+    zends,
     row_flux,
     part,
     sums_x,
@@ -128,6 +139,9 @@
     still,
     first_out,
     slots,
+    ring_d,
+    edge_d,
+    edge_s,
     edge_rows,
     edges_out,
     edges,
@@ -155,7 +169,7 @@
 ):
     mx = lax.axis_index("bx")
     my = lax.axis_index("by")
-    pending = []
+    pending, pending_rims = [], []
 
     def peer(dx, dy):
         return (lax.rem(mx + dx + nx, nx), lax.rem(my + dy + ny, ny))
@@ -167,6 +181,33 @@
         copy.start()
         pending.append(copy)
         return copy
+
+    def send_rim(src, dst, send_sem, recv_sem, dx, dy):
+        copy = pltpu.make_async_remote_copy(
+            src_ref=src, dst_ref=dst, send_sem=send_sem, recv_sem=recv_sem, device_id=peer(dx, dy), device_id_type=MESH
+        )
+        goes, comes = {1: (has_n, has_s), -1: (has_s, has_n), 0: (None, None)}[dy]
+
+        def guarded(action, guard):
+            action() if guard is None else pl.when(guard)(action)
+
+        guarded(copy.start, goes)
+        pending_rims.append(lambda: guarded(copy.wait_send, goes))
+        return lambda: guarded(copy.wait_recv, comes)
+
+    has_n, has_s = my < ny - 1, my > 0
+    barrier = pltpu.get_barrier_semaphore()
+
+    def greet(dx, dy):
+        pl.semaphore_signal(barrier, inc=1, device_id=peer(dx, dy), device_id_type=MESH)
+
+    for off in sorted(range(1, ny), key=lambda o: -min(o, ny - o)):
+        greet(0, off)
+    for off in sorted(range(1, nx), key=lambda o: -min(o, nx - o)):
+        greet(off, 0)
+    for dx, dy in SIDES[4:]:
+        pl.when(has_n if dy == 1 else has_s)(functools.partial(greet, dx, dy))
+    n_peers = nx - 1 + ny - 1 + jnp.where(has_n, 2, 0) + jnp.where(has_s, 2, 0)
 
     last_cols = (slice(None), slice(None), pl.ds(COLS - 128, 128))
     other_cols = (slice(None), slice(None), pl.ds(0, COLS - 128))
@@ -186,12 +227,15 @@
     for copy in loads:
         copy.start()
 
-    barrier = pltpu.get_barrier_semaphore()
-    peers = [peer(dx, dy) for dx, dy in SIDES]
-    peers += [peer(off, 0) for off in range(2, nx - 1)]
-    peers += [peer(0, off) for off in range(2, ny - 1)]
-    for target in peers:
-        pl.semaphore_signal(barrier, inc=1, device_id=target, device_id_type=MESH)
+    def no_rim(at, corners):
+        zrim_row[at] = jnp.zeros((8, COLS), F32)
+        krim_row[at] = jnp.zeros((8, COLS), jnp.int32)
+        for i in corners:
+            zrim_corner[i] = jnp.zeros((8, 128), F32)
+            krim_corner[i] = jnp.zeros((8, 128), jnp.int32)
+
+    pl.when(jnp.logical_not(has_s))(lambda: no_rim(0, (0, 1)))
+    pl.when(jnp.logical_not(has_n))(lambda: no_rim(1, (2, 3)))
 
     loads[0].wait()
     sub = lax.broadcasted_iota(jnp.int32, (8, COLS), 0)
@@ -225,17 +269,20 @@
         both = jnp.where(slot == -2, turned(u0[k, :, COLS - 128 : COLS], 8 * k - 1), turned(ends(c0, k), 8 * k))
         packed = jnp.where(group == k, both, packed)
     col_send[...] = packed
-    pl.semaphore_wait(barrier, len(peers))
-    from_s = send(up_send, up_recv, rs.at[0], rr.at[0], 0, 1)
-    from_n = send(dn_send, dn_recv, rs.at[1], rr.at[1], 0, -1)
-    from_w = send(col_send, col_recv.at[0], rs.at[2], rr.at[2], 1, 0)
-    from_e = send(col_send, col_recv.at[1], rs.at[3], rr.at[3], -1, 0)
+    pl.semaphore_wait(barrier, n_peers)
+    from_s = send_rim(up_send, up_recv, rs.at[0], rr.at[0], 0, 1)
+    from_n = send_rim(dn_send, dn_recv, rs.at[1], rr.at[1], 0, -1)
+    from_w = send_rim(col_send, col_recv.at[0], rs.at[2], rr.at[2], 1, 0)
+    from_e = send_rim(col_send, col_recv.at[1], rs.at[3], rr.at[3], -1, 0)
 
     def rim_refs(row, col, corner):
         return [row.at[0], row.at[1], col.at[0], col.at[1]] + [corner.at[i] for i in range(4)]
 
     k_rims = rim_refs(krim_row, krim_col, krim_corner)
-    k_sends = [send(rim(kmt, s), k_rims[s], ks.at[s], kr.at[s], *SIDES[s]) for s in range(8)]
+    kends[...] = pack_ends(k_x)
+    k_sends = [
+        send_rim(kends if SIDES[s][1] == 0 else rim(kmt, s), k_rims[s], ks.at[s], kr.at[s], *SIDES[s]) for s in range(8)
+    ]
 
     def advance(get, k, put):
         def north_flux(r, c, up, nxt):
@@ -273,9 +320,15 @@
     for copy in loads[6:]:
         copy.wait()
     lax.fori_loop(0, levels, first_step, 0)
-
-    for copy in k_sends:
-        copy.wait_recv()
+    packed = jnp.zeros((ROWS, 128), F32)
+    for k in range(levels):
+        rows_own[0, k : k + 1, :] = c1[k, ROWS - 1 : ROWS, :]
+        rows_own[1, k : k + 1, :] = c1[k, 0:1, :]
+        packed = jnp.where(group == k, turned(ends(c1, k), 8 * k), packed)
+    cols_own[...] = packed
+
+    for arrival in k_sends:
+        arrival()
     extend(k_x, k_rims)
     level16 = lax.broadcasted_iota(jnp.int32, (levels, COLS), 0)
     wet_n = jnp.minimum(k_x[ROWS - 1 : ROWS, 0:COLS], k_x[ROWS : ROWS + 1, 0:COLS]) > level16
@@ -296,8 +349,8 @@
         into = face(turned(col_recv[0], 2), turned(westward, 1), own, wet_w)
         return jnp.where(slot == -1, -out, jnp.where(slot == 0, into, 0.0))
 
-    for copy in (from_s, from_n, from_w, from_e):
-        copy.wait_recv()
+    for arrival in (from_s, from_n, from_w, from_e):
+        arrival()
     rim_rows(dn_recv[...], up_recv[0], up_send[0], dn_send[...])
     flux_cols = rim_cols(col_send[...], col_recv[0], col_recv[1])
 
@@ -308,17 +361,27 @@
         field[k, 0:1, :] = field[k, 0:1, :] + row_flux[1, k : k + 1, :]
         field[k, ROWS - 1 : ROWS, :] = field[k, ROWS - 1 : ROWS, :] - row_flux[0, k : k + 1, :]
 
-    packed = jnp.zeros((ROWS, 128), F32)
+    lane16 = lax.broadcasted_iota(jnp.int32, (levels, 128), 1)
+    level8 = 8 * level16[:, 0:128]
+    on_west, on_east = lane16 == level8, lane16 == ((level8 + 127) & 127)
+    for at, row, sign in ((0, ROWS - 1, -1.0), (1, 0, 1.0)):
+        line = jnp.broadcast_to(flux_cols[row : row + 1, :], (levels, 128))
+        from_west = jnp.sum(jnp.where(on_west, line, 0.0), axis=1, keepdims=True)
+        from_east = jnp.sum(jnp.where(on_east, line, 0.0), axis=1, keepdims=True)
+        change = sign * row_flux[at]
+        value = rows_own[at] + change
+        rows1[at, :, 0:128] = value[:, 0:128] + jnp.where(lane16 == 0, from_west, 0.0)
+        rows1[at, :, 128 : COLS - 128] = value[:, 128 : COLS - 128]
+        rows1[at, :, COLS - 128 : COLS] = value[:, COLS - 128 : COLS] + jnp.where(lane16 == 127, from_east, 0.0)
+        corner = jnp.where(on_west, change[:, 0:1], 0.0) + jnp.where(on_east, change[:, COLS - 1 : COLS], 0.0)
+        cols_own[row : row + 1, :] = cols_own[row : row + 1, :] + jnp.sum(corner, axis=0, keepdims=True)
+    cols1[...] = cols_own[...] + flux_cols
+    from_s = send_rim(rows1.at[0], rows1_recv.at[0], rs.at[4], rr.at[4], 0, 1)
+    from_n = send_rim(rows1.at[1], rows1_recv.at[1], rs.at[5], rr.at[5], 0, -1)
+    from_w = send_rim(cols1, cols1_recv.at[0], rs.at[6], rr.at[6], 1, 0)
+    from_e = send_rim(cols1, cols1_recv.at[1], rs.at[7], rr.at[7], -1, 0)
     for k in range(levels):
         correct(c1, k, flux_cols)
-        rows1[0, k : k + 1, :] = c1[k, ROWS - 1 : ROWS, :]
-        rows1[1, k : k + 1, :] = c1[k, 0:1, :]
-        packed = jnp.where(group == k, turned(ends(c1, k), 8 * k), packed)
-    cols1[...] = packed
-    from_s = send(rows1.at[0], rows1_recv.at[0], rs.at[4], rr.at[4], 0, 1)
-    from_n = send(rows1.at[1], rows1_recv.at[1], rs.at[5], rr.at[5], 0, -1)
-    from_w = send(cols1, cols1_recv.at[0], rs.at[6], rr.at[6], 1, 0)
-    from_e = send(cols1, cols1_recv.at[1], rs.at[7], rr.at[7], -1, 0)
 
     subx = lax.broadcasted_iota(jnp.int32, (8, XC), 0)
     for r in range(STRIPS + 1):
@@ -377,8 +440,8 @@
 
     lax.fori_loop(0, levels, second_step, 0)
 
-    for copy in (from_s, from_n, from_w, from_e):
-        copy.wait_recv()
+    for arrival in (from_s, from_n, from_w, from_e):
+        arrival()
     rim_rows(rows1_recv[1], rows1_recv[0], rows1[0], rows1[1])
     flux_cols = rim_cols(cols1[...], cols1_recv[0], cols1_recv[1])
     dz_rows = jnp.zeros((levels, 128), F32)
@@ -399,7 +462,11 @@
         start = jnp.where(k_x[strip(r), 0:COLS] > 0, rhs[strip(r), :], 0.0)
         basis[0, strip(r), 0:COLS] = start * inv[strip(r), 0:COLS]
     z_rims = rim_refs(zrim_row, zrim_col, zrim_corner)
-    z_sends = [send(rim(basis.at[0], s), z_rims[s], zs.at[s], zr.at[s], *SIDES[s]) for s in range(8)]
+    zends[...] = pack_ends(basis.at[0])
+    z_sends = [
+        send_rim(zends if SIDES[s][1] == 0 else rim(basis.at[0], s), z_rims[s], zs.at[s], zr.at[s], *SIDES[s])
+        for s in range(8)
+    ]
     first_copies = scatter(
         lambda m, i: basis[0, 0:ROWS, block(m)], 1, first_out, lambda off: slots.at[off, pl.ds(0, 1)], fs, fr
     )
@@ -407,8 +474,30 @@
         correct(c2, k, flux_cols)
     write = pltpu.make_async_copy(c2, tracer_out, out_sem)
     write.start()
-    for copy in z_sends:
-        copy.wait_recv()
+
+    lane8 = lax.broadcasted_iota(jnp.int32, (8, BS), 1)
+
+    def pack(both):
+        packed = jnp.zeros((8, BS), F32)
+        for m in range(blocks):
+            packed = jnp.where(((lane8 + 8) & 127) >> 4 == m, turned(both[m], 16 * m), packed)
+        return packed
+
+    def tiles(ref, r):
+        return [ref[strip(r), block(m)] for m in range(blocks + 1)]
+
+    def pack_ring(tile):
+        return pack([jnp.where(lane8 < 64, tile[m + 1], tile[m - 1]) for m in range(blocks)])
+
+    def pack_edges(tile):
+        return pack([jnp.where(lane8 == 0, turned(tile[m], 1), turned(tile[m], -1)) for m in range(blocks)])
+
+    for r in range(STRIPS):
+        ring_d[strip(r), :] = pack_ring(tiles(depth, r))
+        edge_d[strip(r), :] = pack_edges(tiles(depth, r))
+        edge_s[strip(r), :] = (0.25 / HALF) * pack_edges(tiles(inv, r))
+    for arrival in z_sends:
+        arrival()
     extend(basis.at[0], z_rims)
 
     moments = [jnp.zeros((8, 128), F32) for _ in range(8)]
@@ -422,13 +511,9 @@
         return total
 
     moments[0] = inner_product(0, 0)
-    lanex = lax.broadcasted_iota(jnp.int32, (8, XC), 1)
-    first_lane = (lanex & (BS - 1)) == 0
-    lane8 = lanex[:, 0:BS]
-    edge_cols = [jnp.zeros((8, BS), F32) for _ in range(blocks)]
     for step in range(ITERS):
-        rows_x, inner_x = spread_rows(lambda r: basis[step, strip(r), :], STRIPS + 1, True)
-        rows_dx, inner_dx = spread_rows(lambda r: depth[strip(r), :] * basis[step, strip(r), :], STRIPS + 1, True)
+        rows_x = spread_rows(lambda r: basis[step, strip(r), :], STRIPS + 1)
+        rows_dx = spread_rows(lambda r: depth[strip(r), :] * basis[step, strip(r), :], STRIPS + 1)
         for r in range(STRIPS + 1):
             d, x = depth[strip(r), :], basis[step, strip(r), :]
             image = d * spread_cols(rows_x[r]) + spread_cols(rows_dx[r]) - 8.0 * (d * x)
@@ -437,19 +522,6 @@
             if step:
                 following = following + following - basis[step - 1, strip(r), :]
             basis[step + 1, strip(r), :] = following
-            if r < STRIPS:
-                near_x = jnp.where(first_lane, pltpu.roll(inner_x[r], 1, 1), pltpu.roll(inner_x[r], XC - 1, 1))
-                near_dx = jnp.where(first_lane, pltpu.roll(inner_dx[r], 1, 1), pltpu.roll(inner_dx[r], XC - 1, 1))
-                edge = scale * (d * near_x + near_dx)
-                for m in range(blocks):
-                    moved = pltpu.roll(edge[:, m * BS : (m + 1) * BS], 16 * r + 2 * step + 1, 1)
-                    edge_cols[m] = jnp.where((lane8 >> 1) == 8 * r + step, moved, edge_cols[m])
-            else:
-                beyond_x, beyond_dx = spread_cols(x), spread_cols(d * x)
-                for row, out, at in ((ROWS - 1, 0, 0), (0, 7, 1)):
-                    scale = (0.25 / HALF) * inv[row : row + 1, :]
-                    edge = scale * (depth[row : row + 1, :] * beyond_x[out : out + 1] + beyond_dx[out : out + 1])
-                    edge_rows[2 * step + at : 2 * step + at + 1, :] = edge[:, 0:COLS]
         moments[2 * step + 1] = inner_product(step, step + 1)
         if step < ITERS - 1:
             moments[2 * step + 2] = inner_product(step + 1, step + 1)
@@ -460,6 +532,25 @@
         mine = jnp.where(row8 == m, jnp.sum(moments[m], axis=0, keepdims=True), mine)
     part[...] = mine
     x_sends = [send(part, sums_x.at[off], xs.at[off], xr.at[off], off, 0) for off in range(1, nx)]
+    edge_cols = [jnp.zeros((8, BS), F32) for _ in range(blocks)]
+    for step in range(ITERS):
+        ring_x = [pack_ring(tiles(basis.at[step], r)) for r in range(STRIPS)]
+        ring_dx = [ring_d[strip(r), :] * ring_x[r] for r in range(STRIPS)]
+        inner_x = spread_rows(lambda r: ring_x[r], STRIPS, False)
+        inner_dx = spread_rows(lambda r: ring_dx[r], STRIPS, False)
+        for r in range(STRIPS):
+            edge = edge_s[strip(r), :] * (edge_d[strip(r), :] * inner_x[r] + inner_dx[r])
+            for m in range(blocks):
+                moved = turned(edge, 16 * r + 2 * step + 1 - 16 * m)
+                edge_cols[m] = jnp.where((lane8 >> 1) == 8 * r + step, moved, edge_cols[m])
+        x = basis[step, strip(STRIPS), :]
+        beyond_x, beyond_dx = spread_cols(x), spread_cols(depth[strip(STRIPS), :] * x)
+        for row, out, at in ((ROWS - 1, 0, 0), (0, 7, 1)):
+            scale = (0.25 / HALF) * inv[row : row + 1, :]
+            edge = scale * (depth[row : row + 1, :] * beyond_x[out : out + 1] + beyond_dx[out : out + 1])
+            edge_rows[2 * step + at : 2 * step + at + 1, :] = edge[:, 0:COLS]
+    for m in range(blocks):
+        edge_cols[m] = jnp.where((lane8 & 1) == 1, turned(edge_cols[m], 1), turned(edge_cols[m], -1))
     edge_copies = scatter(
         lambda m, i: edge_cols[m] if i else edge_rows[:, block(m)], 2, edges_out, lambda off: edges.at[off], es, er
     )
@@ -578,6 +669,8 @@
     write.wait()
     for copy in pending:
         copy.wait_send()
+    for departure in pending_rims:
+        departure()
 
 
 def on_device(tracer, u_east, v_north, kmt, dest, dz, wind):
@@ -595,7 +688,7 @@
     def rims(dtype):
         return [
             pltpu.VMEM((2, 8, COLS), dtype),
-            pltpu.VMEM((2, ROWS, 128), dtype),
+            pltpu.VMEM((2, 8, 128), dtype),
             pltpu.VMEM((4, 8, 128), dtype),
         ]
 
@@ -604,7 +697,8 @@
     scratch += [pltpu.SMEM(dest.shape, jnp.int32), pltpu.SMEM(dz.shape, F32)]
     scratch += rims(F32) + rims(jnp.int32)
     scratch += [rows2, rows, cols, rows2, rows, cols2]
-    scratch += [rows2, rows2, cols, cols2, rows2]
+    scratch += [rows2, rows2, cols, cols2, rows2, cols]
+    scratch += [pltpu.VMEM((8, 128), jnp.int32), pltpu.VMEM((8, 128), F32), rows2]
     scratch += [
         pltpu.VMEM((8, 128), F32),
         pltpu.VMEM((nx, 8, 128), F32),
@@ -614,6 +708,9 @@
         pltpu.VMEM((nx, 2, ROWS, BS), F32),
         pltpu.VMEM((nx, 1, ROWS, BS), F32),
         pltpu.VMEM((nx, ITERS + 1, ROWS, BS), F32),
+        cols,
+        cols,
+        cols,
         pltpu.VMEM((8, COLS), F32),
         pltpu.VMEM((nx, 2, 8, BS), F32),
         pltpu.VMEM((nx, 2, 8, BS), F32),

time: 40.9 us -> 37 us (0.905)
  Pallas kernels: 38 us -> 34.1 us
    pallas_call x1, Pallas kernels: 38 us -> 34.1 us  [on_device(): pl.pallas_call(functools.partial(kernel, nx, ny, levels), out_shape=(jax....]
where the time goes in v4:
time: 37 us; the launch traced here: 36.9 us
  Pallas kernels  34.1 us (92%)
  local copies, waits for them, and re-layouts  2.11 us (6%)
  between operations  0.64 us (2%)
    pallas_call x1, Pallas kernels, on_device(): pl.pallas_call(functools.partial(kernel, nx, ny, levels), out_shape=(jax....  34.1 us
    unnamed x2, local copies, waits for them, and re-layouts  2.11 us

profile of v4, /device:TPU:1, one launch (start us, length us, event | category | flops | bytes accessed | tf_op | source)
XLA Modules:
  0.0 36.9 jit_solution(16108194037073230594)
XLA Ops:
  0.6 34.1 %shard_map.86 = (f32[16,64,512]{2,1,0:T(8,128)S(1)}, f32[2,64,1024]{2,1,0:T(8,128)S(1)}) custom-call(f32[16,64,512]{2,1,0:T(8,128)} %tracer.1, f32[16,64,512]{2,1,0:T(8,128)} %u_east.1, f32[16,64,512]{2,1,0:T(8,128)} %v_north.1, s32[64,512]{1,0:T(8,128)} %kmt.1, s32[1,4]{1,0:T(1,128)} %dest_in.1, f32[16]{0:T(128)} %dz_in.1, f32[64,512]{1,0:T(8,128)} %wind.1), custom_call_target="tpu_custom_call" | custom-call | tf_op jit(solution)/shard_map/pallas_call | solution.py:724
  34.8 1.3 %copy.11 = f32[16,64,512]{2,1,0:T(8,128)} copy(f32[16,64,512]{2,1,0:T(8,128)S(1)} %get-tuple-element.4) | data formatting | bytes 4194304
  36.1 0.8 %copy.12 = f32[2,64,1024]{2,1,0:T(8,128)} copy(f32[2,64,1024]{2,1,0:T(8,128)S(1)} %get-tuple-element.5) | data formatting | bytes 1048576

commit v5 on v4

--- a/solution.py
+++ b/solution.py
@@ -145,6 +145,9 @@
     edge_rows,
     edges_out,
     edges,
+    edge_rows0,
+    edges0_out,
+    edges0,
     full,
     stage,
     load_sem,
@@ -165,6 +168,8 @@
     fr,
     es,
     er,
+    gs,
+    gr,
     last_sem,
 ):
     mx = lax.axis_index("bx")
@@ -426,7 +431,68 @@
         return pl.ds(m * BS, BS)
 
     still_copies = scatter(
-        lambda m, i: (depth, inv)[i][0:ROWS, block(m)], 2, still_out, lambda off: still.at[off], ds, dr
+        lambda m, i: depth[0:ROWS, block(m)], 1, still_out, lambda off: still.at[off, pl.ds(0, 1)], ds, dr
+    )
+
+    lane8 = lax.broadcasted_iota(jnp.int32, (8, BS), 1)
+
+    def pack(both):
+        packed = jnp.zeros((8, BS), F32)
+        for m in range(blocks):
+            packed = jnp.where(((lane8 + 8) & 127) >> 4 == m, turned(both[m], 16 * m), packed)
+        return packed
+
+    def tiles(ref, r):
+        return [ref[strip(r), block(m)] for m in range(blocks + 1)]
+
+    def pack_ring(tile):
+        return pack([jnp.where(lane8 < 64, tile[m + 1], tile[m - 1]) for m in range(blocks)])
+
+    def pack_edges(tile):
+        return pack([jnp.where(lane8 == 0, turned(tile[m], 1), turned(tile[m], -1)) for m in range(blocks)])
+
+    for r in range(STRIPS):
+        ring_d[strip(r), :] = pack_ring(tiles(depth, r))
+        edge_d[strip(r), :] = pack_edges(tiles(depth, r))
+        edge_s[strip(r), :] = (0.25 / HALF) * pack_edges(tiles(inv, r))
+
+    def edge_columns(step, ring_x, ring_dx, scale, cols_m):
+        inner_x = spread_rows(lambda r: ring_x[r], STRIPS, False)
+        inner_dx = spread_rows(lambda r: ring_dx[r], STRIPS, False)
+        for r in range(STRIPS):
+            edge = scale(r) * (edge_d[strip(r), :] * inner_x[r] + inner_dx[r])
+            for m in range(blocks):
+                moved = turned(edge, 16 * r + 2 * step + 1 - 16 * m)
+                cols_m[m] = jnp.where((lane8 >> 1) == 8 * r + step, moved, cols_m[m])
+
+    def edge_lines(step, x, dx, scale, out_rows):
+        beyond_x, beyond_dx = spread_cols(x), spread_cols(dx)
+        for row, out, at in ((ROWS - 1, 0, 0), (0, 7, 1)):
+            edge = scale(row) * (depth[row : row + 1, :] * beyond_x[out : out + 1] + beyond_dx[out : out + 1])
+            out_rows[2 * step + at : 2 * step + at + 1, :] = edge[:, 0:COLS]
+
+    def swapped(value):
+        return jnp.where((lane8 & 1) == 1, turned(value, 1), turned(value, -1))
+
+    def one_if(wet):
+        return jnp.where(wet, 1.0, 0.0).astype(F32)
+
+    ring_0 = [ring_d[strip(r), :] for r in range(STRIPS)]
+    edge_cols = [jnp.zeros((8, BS), F32) for _ in range(blocks)]
+    edge_columns(
+        0, [one_if(v > 0.0) for v in ring_0], ring_0, lambda r: 0.25 * one_if(edge_d[strip(r), :] > 0.0), edge_cols
+    )
+    edge_rows0[...] = jnp.zeros((8, COLS), F32)
+    edge_lines(
+        0,
+        ocean_of(STRIPS),
+        depth[strip(STRIPS), :],
+        lambda row: 0.25 * one_if(depth[row : row + 1, :] > 0.0),
+        edge_rows0,
+    )
+    edge_cols0 = [swapped(v) for v in edge_cols]
+    edge0_copies = scatter(
+        lambda m, i: edge_cols0[m] if i else edge_rows0[:, block(m)], 2, edges0_out, lambda off: edges0.at[off], gs, gr
     )
 
     def second_step(k, carry):
@@ -475,27 +541,39 @@
     write = pltpu.make_async_copy(c2, tracer_out, out_sem)
     write.start()
 
-    lane8 = lax.broadcasted_iota(jnp.int32, (8, BS), 1)
-
-    def pack(both):
-        packed = jnp.zeros((8, BS), F32)
-        for m in range(blocks):
-            packed = jnp.where(((lane8 + 8) & 127) >> 4 == m, turned(both[m], 16 * m), packed)
-        return packed
-
-    def tiles(ref, r):
-        return [ref[strip(r), block(m)] for m in range(blocks + 1)]
-
-    def pack_ring(tile):
-        return pack([jnp.where(lane8 < 64, tile[m + 1], tile[m - 1]) for m in range(blocks)])
-
-    def pack_edges(tile):
-        return pack([jnp.where(lane8 == 0, turned(tile[m], 1), turned(tile[m], -1)) for m in range(blocks)])
-
-    for r in range(STRIPS):
-        ring_d[strip(r), :] = pack_ring(tiles(depth, r))
-        edge_d[strip(r), :] = pack_edges(tiles(depth, r))
-        edge_s[strip(r), :] = (0.25 / HALF) * pack_edges(tiles(inv, r))
+    for copy in still_copies + edge0_copies:
+        copy.wait_recv()
+    sub8 = lax.broadcasted_iota(jnp.int32, (8, BS), 0)
+    sides = (lane8 == 0) | (lane8 == BS - 1)
+
+    def spread(values):
+        out = []
+        for v in spread_rows(lambda r: values[r], STRIPS, False):
+            east = jnp.where(lane8 == BS - 1, 0.0, pltpu.roll(v, BS - 1, 1))
+            out.append(v + v + (east + jnp.where(lane8 == 0, 0.0, pltpu.roll(v, 1, 1))))
+        return out
+
+    def with_edges(value, r, step, packet, n):
+        value = value + jnp.where(sides, pltpu.roll(packet[n, 1], BS - (16 * r + 2 * step + 1), 1), 0.0)
+        if r == STRIPS - 1:
+            value = value + jnp.where(sub8 == 7, packet[n, 0, 2 * step : 2 * step + 1, :], 0.0)
+        if r == 0:
+            value = value + jnp.where(sub8 == 0, packet[n, 0, 2 * step + 1 : 2 * step + 2, :], 0.0)
+        return value
+
+    def block_diagonal(n, carry):
+        d = [still[n, 0, strip(r), :] for r in range(STRIPS)]
+        o = [one_if(v > 0.0) for v in d]
+        wide_o, wide_d = spread(o), spread(d)
+        for r in range(STRIPS):
+            total = d[r] * wide_o[r] + wide_d[r] - 8.0 * d[r]
+            whole = with_edges(SIGMA + 0.25 * o[r] * total, r, 0, edges0, n)
+            full[n, strip(r), :] = whole
+            still[n, 1, strip(r), :] = o[r] / whole
+        return carry
+
+    lax.fori_loop(0, nx, block_diagonal, 0)
+
     for arrival in z_sends:
         arrival()
     extend(basis.at[0], z_rims)
@@ -536,21 +614,12 @@
     for step in range(ITERS):
         ring_x = [pack_ring(tiles(basis.at[step], r)) for r in range(STRIPS)]
         ring_dx = [ring_d[strip(r), :] * ring_x[r] for r in range(STRIPS)]
-        inner_x = spread_rows(lambda r: ring_x[r], STRIPS, False)
-        inner_dx = spread_rows(lambda r: ring_dx[r], STRIPS, False)
-        for r in range(STRIPS):
-            edge = edge_s[strip(r), :] * (edge_d[strip(r), :] * inner_x[r] + inner_dx[r])
-            for m in range(blocks):
-                moved = turned(edge, 16 * r + 2 * step + 1 - 16 * m)
-                edge_cols[m] = jnp.where((lane8 >> 1) == 8 * r + step, moved, edge_cols[m])
+        edge_columns(step, ring_x, ring_dx, lambda r: edge_s[strip(r), :], edge_cols)
         x = basis[step, strip(STRIPS), :]
-        beyond_x, beyond_dx = spread_cols(x), spread_cols(depth[strip(STRIPS), :] * x)
-        for row, out, at in ((ROWS - 1, 0, 0), (0, 7, 1)):
-            scale = (0.25 / HALF) * inv[row : row + 1, :]
-            edge = scale * (depth[row : row + 1, :] * beyond_x[out : out + 1] + beyond_dx[out : out + 1])
-            edge_rows[2 * step + at : 2 * step + at + 1, :] = edge[:, 0:COLS]
-    for m in range(blocks):
-        edge_cols[m] = jnp.where((lane8 & 1) == 1, turned(edge_cols[m], 1), turned(edge_cols[m], -1))
+        edge_lines(
+            step, x, depth[strip(STRIPS), :] * x, lambda row: (0.25 / HALF) * inv[row : row + 1, :], edge_rows
+        )
+    edge_cols = [swapped(v) for v in edge_cols]
     edge_copies = scatter(
         lambda m, i: edge_cols[m] if i else edge_rows[:, block(m)], 2, edges_out, lambda off: edges.at[off], es, er
     )
@@ -561,28 +630,12 @@
     part2[...] = total
     y_sends = [send(part2, sums_y.at[off], ys.at[off], yr.at[off], 0, off) for off in range(1, ny)]
 
-    for copy in still_copies + first_copies + edge_copies:
+    for copy in first_copies + edge_copies:
         copy.wait_recv()
 
     def repeat(n, carry):
-        sub8 = lax.broadcasted_iota(jnp.int32, (8, BS), 0)
-        zero8 = jnp.zeros((8, BS), F32)
-        sides = (lane8 == 0) | (lane8 == BS - 1)
-
-        def spread(values):
-            up = [pltpu.roll(v, 7, 0) for v in values]
-            down = [pltpu.roll(v, 1, 0) for v in values]
-            out = []
-            for r in range(STRIPS):
-                north = jnp.where(sub8 == 7, up[r + 1] if r + 1 < STRIPS else 0.0, up[r])
-                south = jnp.where(sub8 == 0, down[r - 1] if r else 0.0, down[r])
-                v = values[r] + values[r] + (north + south)
-                east = jnp.where(lane8 == BS - 1, 0.0, pltpu.roll(v, BS - 1, 1))
-                out.append(v + v + (east + jnp.where(lane8 == 0, 0.0, pltpu.roll(v, 1, 1))))
-            return out
-
         x = [slots[n, 0, strip(r), :] for r in range(STRIPS)]
-        before = [zero8] * STRIPS
+        before = x
         for step in range(ITERS):
             dx = [still[n, 0, strip(r), :] * x[r] for r in range(STRIPS)]
             wide_x, wide_dx = spread(x), spread(dx)
@@ -590,20 +643,12 @@
             for r in range(STRIPS):
                 image = still[n, 0, strip(r), :] * wide_x[r] + wide_dx[r] - 8.0 * dx[r]
                 following = (0.25 / HALF) * still[n, 1, strip(r), :] * image - (CENTRE / HALF) * x[r]
-                around = pltpu.roll(edges[n, 1], BS - (16 * r + 2 * step + 1), 1)
-                following = following + jnp.where(sides, around, 0.0)
-                if r == STRIPS - 1:
-                    following = following + jnp.where(sub8 == 7, edges[n, 0, 2 * step : 2 * step + 1, :], 0.0)
-                if r == 0:
-                    following = following + jnp.where(sub8 == 0, edges[n, 0, 2 * step + 1 : 2 * step + 2, :], 0.0)
+                following = with_edges(following, r, step, edges, n)
                 if step:
                     following = following + following - before[r]
                 slots[n, step + 1, strip(r), :] = following
                 after.append(following)
             before, x = x, after
-        for r in range(STRIPS):
-            scaled = still[n, 1, strip(r), :]
-            full[n, strip(r), :] = jnp.where(scaled > 0.0, 1.0 / jnp.where(scaled > 0.0, scaled, 1.0), 0.0)
         return carry
 
     lax.fori_loop(0, nx, repeat, 0)
@@ -704,7 +749,7 @@
         pltpu.VMEM((nx, 8, 128), F32),
         pltpu.VMEM((8, 128), F32),
         pltpu.VMEM((ny, 8, 128), F32),
-        pltpu.VMEM((nx, 2, ROWS, BS), F32),
+        pltpu.VMEM((nx, 1, ROWS, BS), F32),
         pltpu.VMEM((nx, 2, ROWS, BS), F32),
         pltpu.VMEM((nx, 1, ROWS, BS), F32),
         pltpu.VMEM((nx, ITERS + 1, ROWS, BS), F32),
@@ -714,10 +759,13 @@
         pltpu.VMEM((8, COLS), F32),
         pltpu.VMEM((nx, 2, 8, BS), F32),
         pltpu.VMEM((nx, 2, 8, BS), F32),
+        pltpu.VMEM((8, COLS), F32),
+        pltpu.VMEM((nx, 2, 8, BS), F32),
+        pltpu.VMEM((nx, 2, 8, BS), F32),
         pltpu.VMEM((nx, ROWS, BS), F32),
         pltpu.VMEM((nx, 2, ROWS, BS), F32),
     ]
-    counts = [9, None] + [8] * 6 + [nx, nx, ny, ny] + [nx] * 7
+    counts = [9, None] + [8] * 6 + [nx, nx, ny, ny] + [nx] * 9
     scratch += [pltpu.SemaphoreType.DMA((n,)) if n else pltpu.SemaphoreType.DMA for n in counts]
     anywhere = pl.BlockSpec(memory_space=pl.ANY)
     hbm = pl.BlockSpec(memory_space=pltpu.HBM)

time: 37 us -> 36.3 us (0.981)
  Pallas kernels: 34.1 us -> 33.5 us
    pallas_call x1, Pallas kernels: 34.1 us -> 33.5 us  [on_device(): pl.pallas_call(functools.partial(kernel, nx, ny, levels), out_shape=(jax....]
where the time goes in v5:
time: 36.3 us; the launch traced here: 36.2 us
  Pallas kernels  33.5 us (92%)
  local copies, waits for them, and re-layouts  2.11 us (6%)
  between operations  0.64 us (2%)
    pallas_call x1, Pallas kernels, on_device(): pl.pallas_call(functools.partial(kernel, nx, ny, levels), out_shape=(jax....  33.5 us
    unnamed x2, local copies, waits for them, and re-layouts  2.11 us

profile of v5, /device:TPU:1, one launch (start us, length us, event | category | flops | bytes accessed | tf_op | source)
XLA Modules:
  0.0 36.2 jit_solution(16388216300500036694)
XLA Ops:
  0.6 33.5 %shard_map.86 = (f32[16,64,512]{2,1,0:T(8,128)S(1)}, f32[2,64,1024]{2,1,0:T(8,128)S(1)}) custom-call(f32[16,64,512]{2,1,0:T(8,128)} %tracer.1, f32[16,64,512]{2,1,0:T(8,128)} %u_east.1, f32[16,64,512]{2,1,0:T(8,128)} %v_north.1, s32[64,512]{1,0:T(8,128)} %kmt.1, s32[1,4]{1,0:T(1,128)} %dest_in.1, f32[16]{0:T(128)} %dz_in.1, f32[64,512]{1,0:T(8,128)} %wind.1), custom_call_target="tpu_custom_call" | custom-call | tf_op jit(solution)/shard_map/pallas_call | solution.py:772
  34.1 1.3 %copy.11 = f32[16,64,512]{2,1,0:T(8,128)} copy(f32[16,64,512]{2,1,0:T(8,128)S(1)} %get-tuple-element.4) | data formatting | bytes 4194304
  35.4 0.8 %copy.12 = f32[2,64,1024]{2,1,0:T(8,128)} copy(f32[2,64,1024]{2,1,0:T(8,128)S(1)} %get-tuple-element.5) | data formatting | bytes 1048576

commit v6 on v5

--- a/solution.py
+++ b/solution.py
@@ -128,6 +128,9 @@
     cols1_recv,
     rows_own,
     cols_own,
+    corner_send,
+    corner_recv,
+    side_recv,
     kends,
     zends,
     row_flux,
@@ -170,6 +173,8 @@
     er,
     gs,
     gr,
+    hs,
+    hr,
     last_sem,
 ):
     mx = lax.axis_index("bx")
@@ -271,9 +276,18 @@
         up_send[0, k : k + 1, :] = c0[k, ROWS - 1 : ROWS, :]
         up_send[1, k : k + 1, :] = v0[k, ROWS - 1 : ROWS, :]
         dn_send[k : k + 1, :] = c0[k, 0:1, :]
+        corner_send[0, 2, k : k + 1, :] = u0[k, ROWS - 1 : ROWS, COLS - 128 : COLS]
+        corner_send[2, 1, k : k + 1, :] = u0[k, 0:1, COLS - 128 : COLS]
         both = jnp.where(slot == -2, turned(u0[k, :, COLS - 128 : COLS], 8 * k - 1), turned(ends(c0, k), 8 * k))
         packed = jnp.where(group == k, both, packed)
     col_send[...] = packed
+    first, last = pl.ds(0, 128), pl.ds(COLS - 128, 128)
+    for i, end in enumerate((last, first)):
+        corner_send[i, 0] = up_send[0, :, end]
+        corner_send[i, 1] = up_send[1, :, end]
+        corner_send[2 + i, 0] = dn_send[:, end]
+    for i, j in ((1, 2), (2, 2), (3, 1), (3, 2)):
+        corner_send[i, j] = jnp.zeros((levels, 128), F32)
     pl.semaphore_wait(barrier, n_peers)
     from_s = send_rim(up_send, up_recv, rs.at[0], rr.at[0], 0, 1)
     from_n = send_rim(dn_send, dn_recv, rs.at[1], rr.at[1], 0, -1)
@@ -288,6 +302,14 @@
     k_sends = [
         send_rim(kends if SIDES[s][1] == 0 else rim(kmt, s), k_rims[s], ks.at[s], kr.at[s], *SIDES[s]) for s in range(8)
     ]
+
+    corner_sends = [
+        send_rim(corner_send.at[i], corner_recv.at[i], hs.at[i], hr.at[i], *SIDES[4 + i]) for i in range(4)
+    ]
+    for i, (a, b) in enumerate(((0, 2), (2, 1), (0, 1), (1, 1))):
+        corner_sends.append(
+            send_rim(corner_send.at[a, b], side_recv.at[i], hs.at[4 + i], hr.at[4 + i], *SIDES[i])
+        )
 
     def advance(get, k, put):
         def north_flux(r, c, up, nxt):
@@ -331,6 +353,12 @@
         rows_own[1, k : k + 1, :] = c1[k, 0:1, :]
         packed = jnp.where(group == k, turned(ends(c1, k), 8 * k), packed)
     cols_own[...] = packed
+    second = [
+        send_rim(rows_own.at[0], rows1_recv.at[0], rs.at[4], rr.at[4], 0, 1),
+        send_rim(rows_own.at[1], rows1_recv.at[1], rs.at[5], rr.at[5], 0, -1),
+        send_rim(cols_own, cols1_recv.at[0], rs.at[6], rr.at[6], 1, 0),
+        send_rim(cols_own, cols1_recv.at[1], rs.at[7], rr.at[7], -1, 0),
+    ]
 
     for arrival in k_sends:
         arrival()
@@ -368,6 +396,7 @@
 
     lane16 = lax.broadcasted_iota(jnp.int32, (levels, 128), 1)
     level8 = 8 * level16[:, 0:128]
+    cols1[...] = cols_own[...] + flux_cols
     on_west, on_east = lane16 == level8, lane16 == ((level8 + 127) & 127)
     for at, row, sign in ((0, ROWS - 1, -1.0), (1, 0, 1.0)):
         line = jnp.broadcast_to(flux_cols[row : row + 1, :], (levels, 128))
@@ -379,12 +408,7 @@
         rows1[at, :, 128 : COLS - 128] = value[:, 128 : COLS - 128]
         rows1[at, :, COLS - 128 : COLS] = value[:, COLS - 128 : COLS] + jnp.where(lane16 == 127, from_east, 0.0)
         corner = jnp.where(on_west, change[:, 0:1], 0.0) + jnp.where(on_east, change[:, COLS - 1 : COLS], 0.0)
-        cols_own[row : row + 1, :] = cols_own[row : row + 1, :] + jnp.sum(corner, axis=0, keepdims=True)
-    cols1[...] = cols_own[...] + flux_cols
-    from_s = send_rim(rows1.at[0], rows1_recv.at[0], rs.at[4], rr.at[4], 0, 1)
-    from_n = send_rim(rows1.at[1], rows1_recv.at[1], rs.at[5], rr.at[5], 0, -1)
-    from_w = send_rim(cols1, cols1_recv.at[0], rs.at[6], rr.at[6], 1, 0)
-    from_e = send_rim(cols1, cols1_recv.at[1], rs.at[7], rr.at[7], -1, 0)
+        cols1[row : row + 1, :] = cols1[row : row + 1, :] + jnp.sum(corner, axis=0, keepdims=True)
     for k in range(levels):
         correct(c1, k, flux_cols)
 
@@ -506,10 +530,56 @@
 
     lax.fori_loop(0, levels, second_step, 0)
 
-    for arrival in (from_s, from_n, from_w, from_e):
+    for arrival in second + corner_sends:
         arrival()
-    rim_rows(rows1_recv[1], rows1_recv[0], rows1[0], rows1[1])
-    flux_cols = rim_cols(cols1[...], cols1_recv[0], cols1_recv[1])
+    c_s, c_n = up_recv[0], dn_recv[...]
+    (c_sw, v_sw, u_sw), (c_se, v_se) = [corner_recv[0, i] for i in range(3)], [corner_recv[1, i] for i in range(2)]
+    (c_nw, u_nw), c_ne = [corner_recv[2, i] for i in range(2)], corner_recv[3, 0]
+    u_s, u_n, v_w, v_e = [side_recv[i] for i in range(4)]
+    south, north, far_w, far_e = XR - 1, ROWS, XC - 1, COLS
+
+    def both_wet(a, b):
+        here, there = [k_x[i : i + 1, j : j + 1] for i, j in (a, b)]
+        return jnp.minimum(here, there) > level16[:, 0:128]
+
+    def as_rows(line, mask):
+        return jnp.sum(jnp.where(mask, jnp.broadcast_to(line, (levels, 128)), 0.0), axis=1, keepdims=True)
+
+    def as_cols(column, mask):
+        return jnp.sum(jnp.where(mask, column, 0.0), axis=0, keepdims=True)
+
+    flux_sw = face(turned(u_sw, 1), turned(c_sw, 1), c_s[:, 0:128], both_wet((south, far_w), (south, 0)))
+    flux_se = face(u_s, c_s[:, COLS - 128 : COLS], turned(c_se, -1), both_wet((south, COLS - 1), (south, far_e)))
+    flux_nw = face(turned(u_nw, 1), turned(c_nw, 1), c_n[:, 0:128], both_wet((north, far_w), (north, 0)))
+    flux_ne = face(u_n, c_n[:, COLS - 128 : COLS], turned(c_ne, -1), both_wet((north, COLS - 1), (north, far_e)))
+
+    def with_corners(row, flux_w, flux_e):
+        middle = row[:, 128 : COLS - 128]
+        west_end = row[:, 0:128] + jnp.where(lane16 == 0, flux_w, 0.0)
+        east_end = row[:, COLS - 128 : COLS] - jnp.where(lane16 == 127, flux_e, 0.0)
+        return jnp.concatenate([west_end, middle, east_end], axis=1)
+
+    row_s = with_corners(rows1_recv[0] - row_flux[1], flux_sw, flux_se)
+    row_n = with_corners(rows1_recv[1] + row_flux[0], flux_nw, flux_ne)
+
+    w_first, w_last = [as_rows(col_recv[0, r : r + 1, :], on_east) for r in (0, ROWS - 1)]
+    e_first, e_last = [as_rows(col_recv[1, r : r + 1, :], on_west) for r in (0, ROWS - 1)]
+    rise_sw = face(v_sw, c_sw, w_first, both_wet((south, far_w), (0, far_w)))[:, 127:128]
+    rise_nw = face(v_w, w_last, c_nw, both_wet((ROWS - 1, far_w), (north, far_w)))[:, 127:128]
+    rise_se = face(v_se, c_se, e_first, both_wet((south, far_e), (0, far_e)))[:, 0:1]
+    rise_ne = face(v_e, e_last, c_ne, both_wet((ROWS - 1, far_e), (north, far_e)))[:, 0:1]
+    row64 = lax.broadcasted_iota(jnp.int32, (ROWS, 128), 0)
+
+    def beyond(arrived, shift, below, above, mask):
+        value = arrived - turned(flux_cols, shift)
+        value = value + jnp.where(row64 == 0, as_cols(below, mask), 0.0)
+        return value - jnp.where(row64 == ROWS - 1, as_cols(above, mask), 0.0)
+
+    col_w = beyond(cols1_recv[0], -1, rise_sw, rise_nw, on_east)
+    col_e = beyond(cols1_recv[1], 1, rise_se, rise_ne, on_west)
+
+    rim_rows(row_n, row_s, rows1[0], rows1[1])
+    flux_cols = rim_cols(cols1[...], col_w, col_e)
     dz_rows = jnp.zeros((levels, 128), F32)
     dz_cols = jnp.zeros((ROWS, 128), F32)
     for k in range(levels):
@@ -743,6 +813,7 @@
     scratch += rims(F32) + rims(jnp.int32)
     scratch += [rows2, rows, cols, rows2, rows, cols2]
     scratch += [rows2, rows2, cols, cols2, rows2, cols]
+    scratch += [pltpu.VMEM((4, 3, levels, 128), F32)] * 2 + [pltpu.VMEM((4, levels, 128), F32)]
     scratch += [pltpu.VMEM((8, 128), jnp.int32), pltpu.VMEM((8, 128), F32), rows2]
     scratch += [
         pltpu.VMEM((8, 128), F32),
@@ -765,7 +836,7 @@
         pltpu.VMEM((nx, ROWS, BS), F32),
         pltpu.VMEM((nx, 2, ROWS, BS), F32),
     ]
-    counts = [9, None] + [8] * 6 + [nx, nx, ny, ny] + [nx] * 9
+    counts = [9, None] + [8] * 6 + [nx, nx, ny, ny] + [nx] * 8 + [8, 8, nx]
     scratch += [pltpu.SemaphoreType.DMA((n,)) if n else pltpu.SemaphoreType.DMA for n in counts]
     anywhere = pl.BlockSpec(memory_space=pl.ANY)
     hbm = pl.BlockSpec(memory_space=pltpu.HBM)

time: 36.3 us -> 37 us (1.019)
  Pallas kernels: 33.5 us -> 34.1 us
    pallas_call x1, Pallas kernels: 33.5 us -> 34.1 us  [on_device(): pl.pallas_call(functools.partial(kernel, nx, ny, levels), out_shape=(jax....]
where the time goes in v6:
time: 37 us; the launch traced here: 36.9 us
  Pallas kernels  34.1 us (92%)
  local copies, waits for them, and re-layouts  2.11 us (6%)
  between operations  0.64 us (2%)
    pallas_call x1, Pallas kernels, on_device(): pl.pallas_call(functools.partial(kernel, nx, ny, levels), out_shape=(jax....  34.1 us
    unnamed x2, local copies, waits for them, and re-layouts  2.11 us

profile of v6, /device:TPU:1, one launch (start us, length us, event | category | flops | bytes accessed | tf_op | source)
XLA Modules:
  0.0 36.9 jit_solution(16055979466555365654)
XLA Ops:
  0.6 34.1 %shard_map.86 = (f32[16,64,512]{2,1,0:T(8,128)S(1)}, f32[2,64,1024]{2,1,0:T(8,128)S(1)}) custom-call(f32[16,64,512]{2,1,0:T(8,128)} %tracer.1, f32[16,64,512]{2,1,0:T(8,128)} %u_east.1, f32[16,64,512]{2,1,0:T(8,128)} %v_north.1, s32[64,512]{1,0:T(8,128)} %kmt.1, s32[1,4]{1,0:T(1,128)} %dest_in.1, f32[16]{0:T(128)} %dz_in.1, f32[64,512]{1,0:T(8,128)} %wind.1), custom_call_target="tpu_custom_call" | custom-call | tf_op jit(solution)/shard_map/pallas_call | solution.py:843
  34.8 1.3 %copy.11 = f32[16,64,512]{2,1,0:T(8,128)} copy(f32[16,64,512]{2,1,0:T(8,128)S(1)} %get-tuple-element.4) | data formatting | bytes 4194304
  36.1 0.8 %copy.12 = f32[2,64,1024]{2,1,0:T(8,128)} copy(f32[2,64,1024]{2,1,0:T(8,128)S(1)} %get-tuple-element.5) | data formatting | bytes 1048576

commit v7 on v5

--- a/solution.py
+++ b/solution.py
@@ -95,7 +95,6 @@
     u0,
     v0,
     c1,
-    c2,
     k_x,
     ke,
     kn,
@@ -105,6 +104,8 @@
     an,
     bn,
     depth,
+    depth_e,
+    depth_w,
     inv,
     diag,
     basis,
@@ -149,9 +150,7 @@
     edges0_out,
     edges0,
     full,
-    stage,
     load_sem,
-    out_sem,
     ks,
     kr,
     rs,
@@ -170,7 +169,6 @@
     er,
     gs,
     gr,
-    last_sem,
 ):
     mx = lax.axis_index("bx")
     my = lax.axis_index("by")
@@ -395,6 +393,8 @@
         for k in range(levels):
             total = total + jnp.where(here > k, dz[k], 0.0)
         depth[strip(r), :] = total
+        depth_e[strip(r), :] = pltpu.roll(total, XC - 1, 1)
+        depth_w[strip(r), :] = pltpu.roll(total, 1, 1)
 
     def ocean_of(r):
         return jnp.where(k_x[strip(r), :] > 0, 1.0, 0.0).astype(F32)
@@ -497,7 +497,7 @@
 
     def second_step(k, carry):
         def put(r, value):
-            c2[k, strip(r), :] = value
+            tracer_out[k, strip(r), :] = value
             wet = k_x[strip(r), 0:COLS] > k
             rhs[strip(r), :] = rhs[strip(r), :] + jnp.where(wet, dz[k] * value, 0.0)
 
@@ -537,9 +537,7 @@
         lambda m, i: basis[0, 0:ROWS, block(m)], 1, first_out, lambda off: slots.at[off, pl.ds(0, 1)], fs, fr
     )
     for k in range(levels):
-        correct(c2, k, flux_cols)
-    write = pltpu.make_async_copy(c2, tracer_out, out_sem)
-    write.start()
+        correct(tracer_out, k, flux_cols)
 
     for copy in still_copies + edge0_copies:
         copy.wait_recv()
@@ -592,9 +590,11 @@
     for step in range(ITERS):
         rows_x = spread_rows(lambda r: basis[step, strip(r), :], STRIPS + 1)
         rows_dx = spread_rows(lambda r: depth[strip(r), :] * basis[step, strip(r), :], STRIPS + 1)
-        for r in range(STRIPS + 1):
+        for r in range(STRIPS + 1 if step < ITERS - 1 else STRIPS):
             d, x = depth[strip(r), :], basis[step, strip(r), :]
-            image = d * spread_cols(rows_x[r]) + spread_cols(rows_dx[r]) - 8.0 * (d * x)
+            image = 2.0 * (d * rows_x[r] + rows_dx[r]) - 8.0 * (d * x)
+            image = image + pltpu.roll(depth_e[strip(r), :] * rows_x[r] + rows_dx[r], 1, 1)
+            image = image + pltpu.roll(depth_w[strip(r), :] * rows_x[r] + rows_dx[r], XC - 1, 1)
             scale = (0.25 / HALF) * inv[strip(r), :]
             following = scale * image - (CENTRE / HALF) * x
             if step:
@@ -699,19 +699,12 @@
             direction = [v + ratio * w for v, w in zip(z, direction + [zero])]
             norm = following
 
-    results = []
     for n in range(nx):
+        place = pl.ds(pl.multiple_of(lax.rem(mx - n + nx, nx) * BS, BS), BS)
         for r in range(STRIPS):
             y = [slots[n, i, strip(r), :] for i in range(ITERS + 1)]
-            stage[n, 0, strip(r), :] = sum(x[i] * y[i] for i in range(ITERS))
-            stage[n, 1, strip(r), :] = full[n, strip(r), :] * sum(z[i] * y[i] for i in range(ITERS + 1))
-        place = pl.ds(pl.multiple_of(lax.rem(mx - n + nx, nx) * BS, BS), BS)
-        copy = pltpu.make_async_copy(stage.at[n], barotropic.at[:, :, place], last_sem.at[n])
-        copy.start()
-        results.append(copy)
-    for copy in results:
-        copy.wait()
-    write.wait()
+            barotropic[0, strip(r), place] = sum(x[i] * y[i] for i in range(ITERS))
+            barotropic[1, strip(r), place] = full[n, strip(r), :] * sum(z[i] * y[i] for i in range(ITERS + 1))
     for copy in pending:
         copy.wait_send()
     for departure in pending_rims:
@@ -737,8 +730,8 @@
             pltpu.VMEM((4, 8, 128), dtype),
         ]
 
-    scratch = [slab] * 5 + [pltpu.VMEM((XR, XC), jnp.int32), flat_i, flat_i, flat] + [slab] * 4
-    scratch += [ext, ext, ext, pltpu.VMEM((ITERS + 1, XR, XC), F32)]
+    scratch = [slab] * 4 + [pltpu.VMEM((XR, XC), jnp.int32), flat_i, flat_i, flat] + [slab] * 4
+    scratch += [ext, ext, ext, ext, ext, pltpu.VMEM((ITERS + 1, XR, XC), F32)]
     scratch += [pltpu.SMEM(dest.shape, jnp.int32), pltpu.SMEM(dz.shape, F32)]
     scratch += rims(F32) + rims(jnp.int32)
     scratch += [rows2, rows, cols, rows2, rows, cols2]
@@ -763,11 +756,10 @@
         pltpu.VMEM((nx, 2, 8, BS), F32),
         pltpu.VMEM((nx, 2, 8, BS), F32),
         pltpu.VMEM((nx, ROWS, BS), F32),
-        pltpu.VMEM((nx, 2, ROWS, BS), F32),
     ]
-    counts = [9, None] + [8] * 6 + [nx, nx, ny, ny] + [nx] * 9
-    scratch += [pltpu.SemaphoreType.DMA((n,)) if n else pltpu.SemaphoreType.DMA for n in counts]
-    anywhere = pl.BlockSpec(memory_space=pl.ANY)
+    counts = [9] + [8] * 6 + [nx, nx, ny, ny] + [nx] * 8
+    scratch += [pltpu.SemaphoreType.DMA((n,)) for n in counts]
+    in_vmem = pl.BlockSpec(memory_space=pltpu.VMEM)
     hbm = pl.BlockSpec(memory_space=pltpu.HBM)
     return pl.pallas_call(
         functools.partial(kernel, nx, ny, levels),
@@ -776,7 +768,7 @@
             jax.ShapeDtypeStruct((2, ROWS, nx * BS), F32),
         ),
         in_specs=[hbm] * 7,
-        out_specs=(anywhere, anywhere),
+        out_specs=(in_vmem, in_vmem),
         scratch_shapes=scratch,
         compiler_params=pltpu.CompilerParams(
             collective_id=0, has_side_effects=True, vmem_limit_bytes=32 * 1024 * 1024

time: 36.3 us -> 36 us (level)
  Pallas kernels: 33.5 us -> 33.1 us
where the time goes in v7:
time: 36 us; the launch traced here: 35.9 us
  Pallas kernels  33.1 us (92%)
  local copies, waits for them, and re-layouts  2.11 us (6%)
  between operations  0.64 us (2%)
    pallas_call x1, Pallas kernels, on_device(): pl.pallas_call(functools.partial(kernel, nx, ny, levels), out_shape=(jax....  33.1 us
    unnamed x2, local copies, waits for them, and re-layouts  2.11 us

profile of v7, /device:TPU:1, one launch (start us, length us, event | category | flops | bytes accessed | tf_op | source)
XLA Modules:
  0.0 35.9 jit_solution(8253950840906996828)
XLA Ops:
  0.6 33.1 %shard_map.86 = (f32[16,64,512]{2,1,0:T(8,128)S(1)}, f32[2,64,1024]{2,1,0:T(8,128)S(1)}) custom-call(f32[16,64,512]{2,1,0:T(8,128)} %tracer.1, f32[16,64,512]{2,1,0:T(8,128)} %u_east.1, f32[16,64,512]{2,1,0:T(8,128)} %v_north.1, s32[64,512]{1,0:T(8,128)} %kmt.1, s32[1,4]{1,0:T(1,128)} %dest_in.1, f32[16]{0:T(128)} %dz_in.1, f32[64,512]{1,0:T(8,128)} %wind.1), custom_call_target="tpu_custom_call" | custom-call | tf_op jit(solution)/shard_map/pallas_call | solution.py:764
  33.8 1.3 %copy.11 = f32[16,64,512]{2,1,0:T(8,128)} copy(f32[16,64,512]{2,1,0:T(8,128)S(1)} %get-tuple-element.4) | data formatting | bytes 4194304
  35.1 0.8 %copy.12 = f32[2,64,1024]{2,1,0:T(8,128)} copy(f32[2,64,1024]{2,1,0:T(8,128)S(1)} %get-tuple-element.5) | data formatting | bytes 1048576

commit v8 on v7

--- a/solution.py
+++ b/solution.py
@@ -578,15 +578,17 @@
 
     moments = [jnp.zeros((8, 128), F32) for _ in range(8)]
 
-    def inner_product(i, j):
-        total = jnp.zeros((8, 128), F32)
+    def inner_products(j, others):
+        totals = [jnp.zeros((8, 128), F32) for _ in others]
         for r in range(STRIPS):
-            product = diag[strip(r), 0:COLS] * basis[i, strip(r), 0:COLS] * basis[j, strip(r), 0:COLS]
-            for m in range(COLS // 128):
-                total = total + product[:, 128 * m : 128 * (m + 1)]
-        return total
-
-    moments[0] = inner_product(0, 0)
+            weighted = diag[strip(r), 0:COLS] * basis[j, strip(r), 0:COLS]
+            for n, i in enumerate(others):
+                product = weighted * basis[i, strip(r), 0:COLS]
+                for m in range(COLS // 128):
+                    totals[n] = totals[n] + product[:, 128 * m : 128 * (m + 1)]
+        return totals
+
+    moments[0] = inner_products(0, [0])[0]
     for step in range(ITERS):
         rows_x = spread_rows(lambda r: basis[step, strip(r), :], STRIPS + 1)
         rows_dx = spread_rows(lambda r: depth[strip(r), :] * basis[step, strip(r), :], STRIPS + 1)
@@ -599,10 +601,12 @@
             following = scale * image - (CENTRE / HALF) * x
             if step:
                 following = following + following - basis[step - 1, strip(r), :]
-            basis[step + 1, strip(r), :] = following
-        moments[2 * step + 1] = inner_product(step, step + 1)
-        if step < ITERS - 1:
-            moments[2 * step + 2] = inner_product(step + 1, step + 1)
+            if step < ITERS - 1:
+                basis[step + 1, strip(r), :] = following
+            else:
+                basis[step + 1, strip(r), 0:COLS] = following[:, 0:COLS]
+        both = [step, step + 1] if step < ITERS - 1 else [step]
+        moments[2 * step + 1 : 2 * step + 1 + len(both)] = inner_products(step + 1, both)
 
     row8 = lax.broadcasted_iota(jnp.int32, (8, 128), 0)
     mine = jnp.zeros((8, 128), F32)

time: 36 us -> 36 us (level)
  no operation moved by 1% of the time
where the time goes in v8:
time: 36 us; the launch traced here: 35.9 us
  Pallas kernels  33.1 us (92%)
  local copies, waits for them, and re-layouts  2.11 us (6%)
  between operations  0.64 us (2%)
    pallas_call x1, Pallas kernels, on_device(): pl.pallas_call(functools.partial(kernel, nx, ny, levels), out_shape=(jax....  33.1 us
    unnamed x2, local copies, waits for them, and re-layouts  2.11 us

profile of v8, /device:TPU:1, one launch (start us, length us, event | category | flops | bytes accessed | tf_op | source)
XLA Modules:
  0.0 35.9 jit_solution(13532197095166167218)
XLA Ops:
  0.6 33.1 %shard_map.86 = (f32[16,64,512]{2,1,0:T(8,128)S(1)}, f32[2,64,1024]{2,1,0:T(8,128)S(1)}) custom-call(f32[16,64,512]{2,1,0:T(8,128)} %tracer.1, f32[16,64,512]{2,1,0:T(8,128)} %u_east.1, f32[16,64,512]{2,1,0:T(8,128)} %v_north.1, s32[64,512]{1,0:T(8,128)} %kmt.1, s32[1,4]{1,0:T(1,128)} %dest_in.1, f32[16]{0:T(128)} %dz_in.1, f32[64,512]{1,0:T(8,128)} %wind.1), custom_call_target="tpu_custom_call" | custom-call | tf_op jit(solution)/shard_map/pallas_call | solution.py:768
  33.7 1.3 %copy.11 = f32[16,64,512]{2,1,0:T(8,128)} copy(f32[16,64,512]{2,1,0:T(8,128)S(1)} %get-tuple-element.4) | data formatting | bytes 4194304
  35.1 0.8 %copy.12 = f32[2,64,1024]{2,1,0:T(8,128)} copy(f32[2,64,1024]{2,1,0:T(8,128)S(1)} %get-tuple-element.5) | data formatting | bytes 1048576

commit v9 on v8

--- a/solution.py
+++ b/solution.py
@@ -531,7 +531,7 @@
     zends[...] = pack_ends(basis.at[0])
     z_sends = [
         send_rim(zends if SIDES[s][1] == 0 else rim(basis.at[0], s), z_rims[s], zs.at[s], zr.at[s], *SIDES[s])
-        for s in range(8)
+        for s in (4, 5, 6, 7, 0, 1, 2, 3)
     ]
     first_copies = scatter(
         lambda m, i: basis[0, 0:ROWS, block(m)], 1, first_out, lambda off: slots.at[off, pl.ds(0, 1)], fs, fr

time: 36 us -> 36.1 us (level)
  no operation moved by 1% of the time
where the time goes in v9:
time: 36.1 us; the launch traced here: 36 us
  Pallas kernels  33.2 us (92%)
  local copies, waits for them, and re-layouts  2.11 us (6%)
  between operations  0.64 us (2%)
    pallas_call x1, Pallas kernels, on_device(): pl.pallas_call(functools.partial(kernel, nx, ny, levels), out_shape=(jax....  33.2 us
    unnamed x2, local copies, waits for them, and re-layouts  2.11 us

profile of v9, /device:TPU:1, one launch (start us, length us, event | category | flops | bytes accessed | tf_op | source)
XLA Modules:
  0.0 36.0 jit_solution(15119757337072275347)
XLA Ops:
  0.6 33.2 %shard_map.86 = (f32[16,64,512]{2,1,0:T(8,128)S(1)}, f32[2,64,1024]{2,1,0:T(8,128)S(1)}) custom-call(f32[16,64,512]{2,1,0:T(8,128)} %tracer.1, f32[16,64,512]{2,1,0:T(8,128)} %u_east.1, f32[16,64,512]{2,1,0:T(8,128)} %v_north.1, s32[64,512]{1,0:T(8,128)} %kmt.1, s32[1,4]{1,0:T(1,128)} %dest_in.1, f32[16]{0:T(128)} %dz_in.1, f32[64,512]{1,0:T(8,128)} %wind.1), custom_call_target="tpu_custom_call" | custom-call | tf_op jit(solution)/shard_map/pallas_call | solution.py:768
  33.9 1.3 %copy.11 = f32[16,64,512]{2,1,0:T(8,128)} copy(f32[16,64,512]{2,1,0:T(8,128)S(1)} %get-tuple-element.4) | data formatting | bytes 4194304
  35.2 0.8 %copy.12 = f32[2,64,1024]{2,1,0:T(8,128)} copy(f32[2,64,1024]{2,1,0:T(8,128)S(1)} %get-tuple-element.5) | data formatting | bytes 1048576
